TPU v7x, 512 devices: a whole 4x4x16 slice. The times are simulated.
512 devices in a mesh: tm: 16 (over z), sta: 32 (over y, x, core).
Axes of the slice: x: 4, y: 4, z: 16, core: 2. Of those that a mesh axis runs over, the one named last changes fastest.
Arguments:
- ray_basis: bfloat16 [16, 32768, 256], P('tm', 'sta'), may hold values from -0.06629126 to 0.06629126
- delays: bfloat16 [16, 32768], P('tm', 'sta'), may hold values from -24 to 24
- ray_station: int32 [16, 32768], P('tm', 'sta'), may hold values from 0 to 511, as said below
- ray_count: int32 [16, 32], P('tm', 'sta'), may hold values from 128 to 1024, as said below
- station_var: float32 [512], P('sta'), may hold values from 0.25 to 4
- decay_factor: float32 [16, 256], P('tm'), may hold values from 0.02 to 0.995, as said below
- mode_variance: float32 [256], replicated, may hold values from 0.3 to 3
- prior_mean: float32 [256], replicated, may hold values from -6 to 6
Outputs:
- smoothed: float32 [16, 256], P('tm')
Inputs may be any that keep to these rules, and one draw needn't show every extreme that they name: `ray_station`: each ray's station is one of the 16 stations of the station shard that holds the ray. `ray_count`: each entry is a multiple of 128; the live slots of a shard come first; some shard is full in every draw. `decay_factor`: each entry lies strictly between 0 and 1.
All inputs are finite; a program needn't handle non-finite values.
Results may differ from a plain program's by a relative error of at most 0.005.
Values sent between devices are 32-bit elements; how exact they have to be, the bound alone decides.
No kernel may reach another device: no remote copies, remote signals or barrier semaphores. Data moves between devices by JAX's collectives and lax.ppermute only.
A program may use at most 64 MiB of HBM per device.

v0:
```python
import jax
import jax.numpy as jnp
from jax import lax
from jax.sharding import PartitionSpec as P

PRECISE = lax.Precision.HIGHEST


def passed_along(x, axis, by):
    devices = lax.axis_size(axis)
    pairs = [(i, i + by) for i in range(devices) if 0 <= i + by < devices]
    return lax.ppermute(x, axis, pairs)


def product(left, right):
    return jnp.dot(left, right, precision=PRECISE)


def spd_inverse(matrix):
    lower_factor = jnp.linalg.cholesky(matrix)
    identity = jnp.eye(matrix.shape[0], dtype=matrix.dtype)
    inverse = jax.scipy.linalg.cho_solve((lower_factor, True), identity)
    return 0.5 * (inverse + inverse.T)


def kalman_update(mean_prev, info_prev, decay_row, noise_row, information, drive_vector, is_first):
    inverse_noise = 1.0 / noise_row
    scaled = decay_row * inverse_noise
    identity = jnp.eye(noise_row.shape[0], dtype=jnp.float32)
    inner = jnp.where(is_first, identity, info_prev + jnp.diag(decay_row * scaled))
    kernel = spd_inverse(inner)
    pred_info = jnp.diag(inverse_noise) - jnp.where(
        is_first, 0.0, scaled[:, None] * kernel * scaled[None, :]
    )
    info_new = pred_info + information
    info_new = 0.5 * (info_new + info_new.T)
    target = product(pred_info, decay_row * mean_prev) + drive_vector
    factor = jnp.linalg.cholesky(info_new)
    mean_new = jax.scipy.linalg.cho_solve((factor, True), target)
    return (mean_new, info_new)


def run_filter(
    mean_prev, info_prev, first_index, decay_factor, process_noise, information, drive_vector
):
    is_first = first_index + 0 == 0
    mean_prev, info_prev = kalman_update(
        mean_prev,
        info_prev,
        decay_factor[0],
        process_noise[0],
        information[0],
        drive_vector[0],
        is_first,
    )
    filtered = [mean_prev]
    infos = [info_prev]
    return (jnp.stack(filtered), jnp.stack(infos))


def run_adjoint(adjoint, filtered, covariances, decay_factor, information, drive_vector):
    smoothed = []
    for position in reversed(range(decay_factor.shape[0])):
        smooth = filtered[position] + product(covariances[position], adjoint)
        adjoint = decay_factor[position] * (
            adjoint + drive_vector[position] - product(information[position], smooth)
        )
        smoothed.append(smooth)
    return (jnp.stack(smoothed[::-1]), adjoint)


def shards(
    ray_basis, delays, ray_station, ray_count, station_var, decay_factor, mode_variance, prior_mean
):
    epochs_here, rays_here, state_width = ray_basis.shape
    stations_here = station_var.shape[0]
    tm_size = lax.axis_size("tm")
    tm_index = lax.axis_index("tm")
    first_index = tm_index * epochs_here
    local_station = ray_station - lax.axis_index("sta") * stations_here
    station_codes = jnp.arange(stations_here, dtype=jnp.int32)
    inverse_var = 1.0 / station_var
    matches = local_station[:, :, None] == station_codes[None, None, :]
    weight = jnp.sum(jnp.where(matches, inverse_var[None, None, :], 0.0), axis=2)
    slot_index = lax.broadcasted_iota(jnp.int32, (epochs_here, rays_here), 1)
    weight = jnp.where(slot_index < ray_count, weight, 0.0)
    weighted = (ray_basis * weight[:, :, None]).astype(jnp.bfloat16)
    info_part = jnp.einsum("ern,erm->enm", weighted, ray_basis, preferred_element_type=jnp.float32)
    drive_part = jnp.einsum("er,ern->en", delays, weighted, preferred_element_type=jnp.float32)
    information, drive_vector = lax.psum((info_part, drive_part), "sta")
    process_noise = (1.0 - decay_factor * decay_factor) * mode_variance[None, :]
    identity = jnp.eye(state_width, dtype=jnp.float32)

    def advance(mean_in, info_in, stored):
        return run_filter(
            mean_in, info_in, first_index, decay_factor, process_noise, information, drive_vector
        )

    def remain(mean_in, info_in, stored):
        return stored

    empty = (
        jnp.zeros((epochs_here, state_width), jnp.float32),
        jnp.zeros((epochs_here, state_width, state_width), jnp.float32),
    )
    stored = lax.cond(tm_index == 0, advance, remain, prior_mean, identity, empty)

    def handoff(turn, stored):
        received = passed_along((stored[0][-1], stored[1][-1]), "tm", 1)
        return lax.cond(tm_index == turn, advance, remain, received[0], received[1], stored)

    filtered, filter_infos = lax.fori_loop(1, tm_size, handoff, stored)
    covariances = jnp.stack([spd_inverse(filter_infos[0])])

    def sweep(adjoint_in, kept):
        return run_adjoint(
            adjoint_in, filtered, covariances, decay_factor, information, drive_vector
        )

    def hold(adjoint_in, kept):
        return kept

    zero_vector = jnp.zeros((state_width,), jnp.float32)
    blank = (jnp.zeros((epochs_here, state_width), jnp.float32), zero_vector)
    kept = lax.cond(tm_index == tm_size - 1, sweep, hold, zero_vector, blank)

    def handback(turn, kept):
        received = passed_along(kept[1], "tm", -1)
        return lax.cond(tm_index == tm_size - 2 - turn, sweep, hold, received, kept)

    smoothed, _ = lax.fori_loop(0, tm_size - 1, handback, kept)
    return smoothed


def solution(mesh):
    placed = (
        P("tm", "sta", None),
        P("tm", "sta"),
        P("tm", "sta"),
        P("tm", "sta"),
        P("sta"),
        P("tm", None),
        P(),
        P(),
    )
    return jax.shard_map(
        shards, mesh=mesh, in_specs=placed, out_specs=P("tm", None), check_vma=False
    )
```

profile of v0, /device:TPU:1, one launch (start us, length us, event | category | flops | bytes accessed | tf_op | source)
XLA Modules:
  0.0 2406.1 jit_solution(8053430109165242259)
XLA Ops:
  11.6 68.9 %psum.15 = f32[1,256]{1,0:T(1,128)S(1)} all-reduce(f32[1,256]{1,0:T(1,128)S(1)} %fusion.79), channel_id=1, replica_groups=mesh['tm'=16,'sta'=32] {'sta'}, use_global_device_ids=true, to_apply=%region_2.3 | all-reduce | flops 256 | bytes 2048 | tf_op jit(solution)/shard_map/psum | solution.py:90
  80.5 67.6 %all-reduce.3.cloned.1.call-done = f32[1,256,256]{2,1,0:T(8,128)} async-done(((f32[1,256,256]{2,1,0:T(8,128)}), f32[1,256,256]{2,1,0:T(8,128)}) %all-reduce.3.cloned.1.call-update) | async-done | bytes 262160 | tf_op jit(solution)/shard_map/psum | solution.py:90
  148.1 126.9 %conditional.4 = (f32[1,256]{1,0:T(1,128)S(1)}, f32[1,256,256]{1,2,0:T(8,128)S(1)}) conditional(s32[]{:T(128)} %convert_element_type.45, () %tuple.67, (f32[1,256]{1,0:T(1,128)S(1)}, s32[]{:T(128)}, f32[1,256]{1,0:T(1,128)S(1)}, f32[256,256]{1,0:T(8,128)S(1)}, f32[1,256,256]{2,1,0:T(8,128)}, /*index=5*/f32[256]{0:T(256)S(1)}, ...), branch_computations={%region_3.4_spmd, %region_4.12_spmd} | conditional | flops 407341824 | bytes 17728998 | solution.py:106
  148.5 11.7 cholesky.256
  188.7 19.9 custom-call.26
  253.5 19.7 custom-call.28
  274.9 1363.4 %while.44 = (s32[]{:T(128)}, f32[1,256]{1,0:T(1,128)S(1)}, f32[1,256,256]{1,2,0:T(8,128)S(1)}, s32[]{:T(128)}, f32[1,256]{1,0:T(1,128)S(1)}, /*index=5*/f32[1,25...) while((s32[]{:T(128)}, f32[1,256]{1,0:T(1,128)S(1)}, ...), condition=%wide.region_12.16_spmd, body=%wide.region_9.15_spmd.sunk | while | flops 407341824 | bytes 19306224 | solution.py:112
  281.7 129.4 %collective-permute-start.1 = (f32[256,256]{1,0:T(8,128)S(1)}, f32[256,256]{1,0:T(8,128)S(1)}, u32[]{:S(2)}, u32[]{:S(2)}) collective-permute-start(f32[256,256]{1,0:T(8,128)S(1)} %bitcast.362), channel_id=1, source_target_pairs={{0,32},{32,64},{64,96},{96,128},{128,160},{160,192},{192,224},{224... | collective-permute-start | bytes 786440 | tf_op jit(solution)/shard_map/while/body/eval_jaxpr/ppermute | solution.py:12
  419.6 127.5 %collective-permute-start.2 = (f32[256]{0:T(256)S(1)}, f32[256]{0:T(256)S(1)}, u32[]{:S(2)}, u32[]{:S(2)}) collective-permute-start(f32[256]{0:T(256)S(1)} %bitcast.383), channel_id=1, source_target_pairs={{0,32},{32,64},{64,96},{96,128},{128,160},{160,192},{192,224},{224... | collective-permute-start | bytes 3080 | tf_op jit(solution)/shard_map/while/body/eval_jaxpr/ppermute | solution.py:12
  555.7 127.5 %collective-permute-start.1 = (f32[256,256]{1,0:T(8,128)S(1)}, f32[256,256]{1,0:T(8,128)S(1)}, u32[]{:S(2)}, u32[]{:S(2)}) collective-permute-start(f32[256,256]{1,0:T(8,128)S(1)} %bitcast.362), channel_id=1, source_target_pairs={{0,32},{32,64},{64,96},{96,128},{128,160},{160,192},{192,224},{224... | collective-permute-start | bytes 786440 | tf_op jit(solution)/shard_map/while/body/eval_jaxpr/ppermute | solution.py:12
  691.3 127.7 %collective-permute-start.2 = (f32[256]{0:T(256)S(1)}, f32[256]{0:T(256)S(1)}, u32[]{:S(2)}, u32[]{:S(2)}) collective-permute-start(f32[256]{0:T(256)S(1)} %bitcast.383), channel_id=1, source_target_pairs={{0,32},{32,64},{64,96},{96,128},{128,160},{160,192},{192,224},{224... | collective-permute-start | bytes 3080 | tf_op jit(solution)/shard_map/while/body/eval_jaxpr/ppermute | solution.py:12
  828.4 126.1 %collective-permute-start.1 = (f32[256,256]{1,0:T(8,128)S(1)}, f32[256,256]{1,0:T(8,128)S(1)}, u32[]{:S(2)}, u32[]{:S(2)}) collective-permute-start(f32[256,256]{1,0:T(8,128)S(1)} %bitcast.362), channel_id=1, source_target_pairs={{0,32},{32,64},{64,96},{96,128},{128,160},{160,192},{192,224},{224... | collective-permute-start | bytes 786440 | tf_op jit(solution)/shard_map/while/body/eval_jaxpr/ppermute | solution.py:12
  963.7 125.3 %collective-permute-start.2 = (f32[256]{0:T(256)S(1)}, f32[256]{0:T(256)S(1)}, u32[]{:S(2)}, u32[]{:S(2)}) collective-permute-start(f32[256]{0:T(256)S(1)} %bitcast.383), channel_id=1, source_target_pairs={{0,32},{32,64},{64,96},{96,128},{128,160},{160,192},{192,224},{224... | collective-permute-start | bytes 3080 | tf_op jit(solution)/shard_map/while/body/eval_jaxpr/ppermute | solution.py:12
  1099.1 125.3 %collective-permute-start.1 = (f32[256,256]{1,0:T(8,128)S(1)}, f32[256,256]{1,0:T(8,128)S(1)}, u32[]{:S(2)}, u32[]{:S(2)}) collective-permute-start(f32[256,256]{1,0:T(8,128)S(1)} %bitcast.362), channel_id=1, source_target_pairs={{0,32},{32,64},{64,96},{96,128},{128,160},{160,192},{192,224},{224... | collective-permute-start | bytes 786440 | tf_op jit(solution)/shard_map/while/body/eval_jaxpr/ppermute | solution.py:12
  1233.7 126.5 %collective-permute-start.2 = (f32[256]{0:T(256)S(1)}, f32[256]{0:T(256)S(1)}, u32[]{:S(2)}, u32[]{:S(2)}) collective-permute-start(f32[256]{0:T(256)S(1)} %bitcast.383), channel_id=1, source_target_pairs={{0,32},{32,64},{64,96},{96,128},{128,160},{160,192},{192,224},{224... | collective-permute-start | bytes 3080 | tf_op jit(solution)/shard_map/while/body/eval_jaxpr/ppermute | solution.py:12
  1370.3 125.3 %collective-permute-start.1 = (f32[256,256]{1,0:T(8,128)S(1)}, f32[256,256]{1,0:T(8,128)S(1)}, u32[]{:S(2)}, u32[]{:S(2)}) collective-permute-start(f32[256,256]{1,0:T(8,128)S(1)} %bitcast.362), channel_id=1, source_target_pairs={{0,32},{32,64},{64,96},{96,128},{128,160},{160,192},{192,224},{224... | collective-permute-start | bytes 786440 | tf_op jit(solution)/shard_map/while/body/eval_jaxpr/ppermute | solution.py:12
  1504.9 125.3 %collective-permute-start.2 = (f32[256]{0:T(256)S(1)}, f32[256]{0:T(256)S(1)}, u32[]{:S(2)}, u32[]{:S(2)}) collective-permute-start(f32[256]{0:T(256)S(1)} %bitcast.383), channel_id=1, source_target_pairs={{0,32},{32,64},{64,96},{96,128},{128,160},{160,192},{192,224},{224... | collective-permute-start | bytes 3080 | tf_op jit(solution)/shard_map/while/body/eval_jaxpr/ppermute | solution.py:12
  1678.4 19.9 custom-call.34
  1701.7 697.3 %while.45 = (s32[]{:T(128)}, f32[1,256]{1,0:T(1,128)}, f32[256]{0:T(256)S(1)}, s32[]{:T(128)}, f32[1,256]{1,0:T(1,128)S(1)}, /*index=5*/f32[256,256]{1,0:T(8,128...) while((s32[]{:T(128)}, f32[1,256]{1,0:T(1,128)}, ...), condition=%wide.region_18.22_spmd, body=%wide.region_15.21_spmd.sunk | while | flops 1573893 | bytes 545059 | solution.py:131
  1713.3 124.9 %collective-permute-done = f32[256]{0:T(256)S(1)} collective-permute-done((f32[256]{0:T(256)S(1)}, f32[256]{0:T(256)S(1)}, u32[]{:S(2)}, u32[]{:S(2)}) %collective-permute-start) | collective-permute-done | bytes 1056 | tf_op jit(solution)/shard_map/while/body/eval_jaxpr/ppermute | solution.py:12
  1850.8 125.2 %collective-permute-done = f32[256]{0:T(256)S(1)} collective-permute-done((f32[256]{0:T(256)S(1)}, f32[256]{0:T(256)S(1)}, u32[]{:S(2)}, u32[]{:S(2)}) %collective-permute-start) | collective-permute-done | bytes 1056 | tf_op jit(solution)/shard_map/while/body/eval_jaxpr/ppermute | solution.py:12
  1988.3 124.2 %collective-permute-done = f32[256]{0:T(256)S(1)} collective-permute-done((f32[256]{0:T(256)S(1)}, f32[256]{0:T(256)S(1)}, u32[]{:S(2)}, u32[]{:S(2)}) %collective-permute-start) | collective-permute-done | bytes 1056 | tf_op jit(solution)/shard_map/while/body/eval_jaxpr/ppermute | solution.py:12
  2125.1 124.0 %collective-permute-done = f32[256]{0:T(256)S(1)} collective-permute-done((f32[256]{0:T(256)S(1)}, f32[256]{0:T(256)S(1)}, u32[]{:S(2)}, u32[]{:S(2)}) %collective-permute-start) | collective-permute-done | bytes 1056 | tf_op jit(solution)/shard_map/while/body/eval_jaxpr/ppermute | solution.py:12
  2261.3 136.7 %collective-permute-done = f32[256]{0:T(256)S(1)} collective-permute-done((f32[256]{0:T(256)S(1)}, f32[256]{0:T(256)S(1)}, u32[]{:S(2)}, u32[]{:S(2)}) %collective-permute-start) | collective-permute-done | bytes 1056 | tf_op jit(solution)/shard_map/while/body/eval_jaxpr/ppermute | solution.py:12
  (294 shorter events, 283.9 us)
Async XLA Ops:
  6.5 141.5 %all-reduce.3.cloned.1.call-start = ((), (), s32[]{:S(2)}) async-start(), calls=%async_computation | async-start | bytes 524288 | tf_op jit(solution)/shard_map/psum | solution.py:90
  281.7 133.6 %collective-permute-start.1 = (f32[256,256]{1,0:T(8,128)S(1)}, f32[256,256]{1,0:T(8,128)S(1)}, u32[]{:S(2)}, u32[]{:S(2)}) collective-permute-start(f32[256,256]{1,0:T(8,128)S(1)} %bitcast.362), channel_id=1, source_target_pairs={{0,32},{32,64},{64,96},{96,128},{128,160},{160,192},{192,224},{224... | collective-permute-start | bytes 786440 | tf_op jit(solution)/shard_map/while/body/eval_jaxpr/ppermute | solution.py:12
  415.4 132.4 %collective-permute-start.1 = (f32[256,256]{1,0:T(8,128)S(1)}, f32[256,256]{1,0:T(8,128)S(1)}, u32[]{:S(2)}, u32[]{:S(2)}) collective-permute-start(f32[256,256]{1,0:T(8,128)S(1)} %bitcast.362), channel_id=1, source_target_pairs={{0,32},{32,64},{64,96},{96,128},{128,160},{160,192},{192,224},{224... | collective-permute-start | bytes 786440 | tf_op jit(solution)/shard_map/while/body/eval_jaxpr/ppermute | solution.py:12
  419.6 128.2 %collective-permute-start.2 = (f32[256]{0:T(256)S(1)}, f32[256]{0:T(256)S(1)}, u32[]{:S(2)}, u32[]{:S(2)}) collective-permute-start(f32[256]{0:T(256)S(1)} %bitcast.383), channel_id=1, source_target_pairs={{0,32},{32,64},{64,96},{96,128},{128,160},{160,192},{192,224},{224... | collective-permute-start | bytes 3080 | tf_op jit(solution)/shard_map/while/body/eval_jaxpr/ppermute | solution.py:12
  555.7 131.9 %collective-permute-start.1 = (f32[256,256]{1,0:T(8,128)S(1)}, f32[256,256]{1,0:T(8,128)S(1)}, u32[]{:S(2)}, u32[]{:S(2)}) collective-permute-start(f32[256,256]{1,0:T(8,128)S(1)} %bitcast.362), channel_id=1, source_target_pairs={{0,32},{32,64},{64,96},{96,128},{128,160},{160,192},{192,224},{224... | collective-permute-start | bytes 786440 | tf_op jit(solution)/shard_map/while/body/eval_jaxpr/ppermute | solution.py:12
  687.7 132.0 %collective-permute-start.1 = (f32[256,256]{1,0:T(8,128)S(1)}, f32[256,256]{1,0:T(8,128)S(1)}, u32[]{:S(2)}, u32[]{:S(2)}) collective-permute-start(f32[256,256]{1,0:T(8,128)S(1)} %bitcast.362), channel_id=1, source_target_pairs={{0,32},{32,64},{64,96},{96,128},{128,160},{160,192},{192,224},{224... | collective-permute-start | bytes 786440 | tf_op jit(solution)/shard_map/while/body/eval_jaxpr/ppermute | solution.py:12
  691.3 128.4 %collective-permute-start.2 = (f32[256]{0:T(256)S(1)}, f32[256]{0:T(256)S(1)}, u32[]{:S(2)}, u32[]{:S(2)}) collective-permute-start(f32[256]{0:T(256)S(1)} %bitcast.383), channel_id=1, source_target_pairs={{0,32},{32,64},{64,96},{96,128},{128,160},{160,192},{192,224},{224... | collective-permute-start | bytes 3080 | tf_op jit(solution)/shard_map/while/body/eval_jaxpr/ppermute | solution.py:12
  819.9 8.4 collective-permute-start.1
  828.4 131.6 %collective-permute-start.1 = (f32[256,256]{1,0:T(8,128)S(1)}, f32[256,256]{1,0:T(8,128)S(1)}, u32[]{:S(2)}, u32[]{:S(2)}) collective-permute-start(f32[256,256]{1,0:T(8,128)S(1)} %bitcast.362), channel_id=1, source_target_pairs={{0,32},{32,64},{64,96},{96,128},{128,160},{160,192},{192,224},{224... | collective-permute-start | bytes 786440 | tf_op jit(solution)/shard_map/while/body/eval_jaxpr/ppermute | solution.py:12
  960.1 129.6 %collective-permute-start.1 = (f32[256,256]{1,0:T(8,128)S(1)}, f32[256,256]{1,0:T(8,128)S(1)}, u32[]{:S(2)}, u32[]{:S(2)}) collective-permute-start(f32[256,256]{1,0:T(8,128)S(1)} %bitcast.362), channel_id=1, source_target_pairs={{0,32},{32,64},{64,96},{96,128},{128,160},{160,192},{192,224},{224... | collective-permute-start | bytes 786440 | tf_op jit(solution)/shard_map/while/body/eval_jaxpr/ppermute | solution.py:12
  963.7 126.0 %collective-permute-start.2 = (f32[256]{0:T(256)S(1)}, f32[256]{0:T(256)S(1)}, u32[]{:S(2)}, u32[]{:S(2)}) collective-permute-start(f32[256]{0:T(256)S(1)} %bitcast.383), channel_id=1, source_target_pairs={{0,32},{32,64},{64,96},{96,128},{128,160},{160,192},{192,224},{224... | collective-permute-start | bytes 3080 | tf_op jit(solution)/shard_map/while/body/eval_jaxpr/ppermute | solution.py:12
  1089.9 9.1 collective-permute-start.1
  1099.1 130.8 %collective-permute-start.1 = (f32[256,256]{1,0:T(8,128)S(1)}, f32[256,256]{1,0:T(8,128)S(1)}, u32[]{:S(2)}, u32[]{:S(2)}) collective-permute-start(f32[256,256]{1,0:T(8,128)S(1)} %bitcast.362), channel_id=1, source_target_pairs={{0,32},{32,64},{64,96},{96,128},{128,160},{160,192},{192,224},{224... | collective-permute-start | bytes 786440 | tf_op jit(solution)/shard_map/while/body/eval_jaxpr/ppermute | solution.py:12
  1230.1 130.8 %collective-permute-start.1 = (f32[256,256]{1,0:T(8,128)S(1)}, f32[256,256]{1,0:T(8,128)S(1)}, u32[]{:S(2)}, u32[]{:S(2)}) collective-permute-start(f32[256,256]{1,0:T(8,128)S(1)} %bitcast.362), channel_id=1, source_target_pairs={{0,32},{32,64},{64,96},{96,128},{128,160},{160,192},{192,224},{224... | collective-permute-start | bytes 786440 | tf_op jit(solution)/shard_map/while/body/eval_jaxpr/ppermute | solution.py:12
  1233.7 127.2 %collective-permute-start.2 = (f32[256]{0:T(256)S(1)}, f32[256]{0:T(256)S(1)}, u32[]{:S(2)}, u32[]{:S(2)}) collective-permute-start(f32[256]{0:T(256)S(1)} %bitcast.383), channel_id=1, source_target_pairs={{0,32},{32,64},{64,96},{96,128},{128,160},{160,192},{192,224},{224... | collective-permute-start | bytes 3080 | tf_op jit(solution)/shard_map/while/body/eval_jaxpr/ppermute | solution.py:12
  1361.1 9.1 collective-permute-start.1
  1370.3 130.8 %collective-permute-start.1 = (f32[256,256]{1,0:T(8,128)S(1)}, f32[256,256]{1,0:T(8,128)S(1)}, u32[]{:S(2)}, u32[]{:S(2)}) collective-permute-start(f32[256,256]{1,0:T(8,128)S(1)} %bitcast.362), channel_id=1, source_target_pairs={{0,32},{32,64},{64,96},{96,128},{128,160},{160,192},{192,224},{224... | collective-permute-start | bytes 786440 | tf_op jit(solution)/shard_map/while/body/eval_jaxpr/ppermute | solution.py:12
  1501.3 129.6 %collective-permute-start.1 = (f32[256,256]{1,0:T(8,128)S(1)}, f32[256,256]{1,0:T(8,128)S(1)}, u32[]{:S(2)}, u32[]{:S(2)}) collective-permute-start(f32[256,256]{1,0:T(8,128)S(1)} %bitcast.362), channel_id=1, source_target_pairs={{0,32},{32,64},{64,96},{96,128},{128,160},{160,192},{192,224},{224... | collective-permute-start | bytes 786440 | tf_op jit(solution)/shard_map/while/body/eval_jaxpr/ppermute | solution.py:12
  1504.9 126.0 %collective-permute-start.2 = (f32[256]{0:T(256)S(1)}, f32[256]{0:T(256)S(1)}, u32[]{:S(2)}, u32[]{:S(2)}) collective-permute-start(f32[256]{0:T(256)S(1)} %bitcast.383), channel_id=1, source_target_pairs={{0,32},{32,64},{64,96},{96,128},{128,160},{160,192},{192,224},{224... | collective-permute-start | bytes 3080 | tf_op jit(solution)/shard_map/while/body/eval_jaxpr/ppermute | solution.py:12
  1712.0 126.2 %collective-permute-start = (f32[256]{0:T(256)S(1)}, f32[256]{0:T(256)S(1)}, u32[]{:S(2)}, u32[]{:S(2)}) collective-permute-start(f32[256]{0:T(256)S(1)} %get-tuple-element.971), channel_id=1, source_target_pairs={{32,0},{64,32},{96,64},{128,96},{160,128},{192,160},{224,192},{256... | collective-permute-start | bytes 3080 | tf_op jit(solution)/shard_map/while/body/eval_jaxpr/ppermute | solution.py:12
  1849.5 126.5 %collective-permute-start = (f32[256]{0:T(256)S(1)}, f32[256]{0:T(256)S(1)}, u32[]{:S(2)}, u32[]{:S(2)}) collective-permute-start(f32[256]{0:T(256)S(1)} %get-tuple-element.971), channel_id=1, source_target_pairs={{32,0},{64,32},{96,64},{128,96},{160,128},{192,160},{224,192},{256... | collective-permute-start | bytes 3080 | tf_op jit(solution)/shard_map/while/body/eval_jaxpr/ppermute | solution.py:12
  1987.0 125.5 %collective-permute-start = (f32[256]{0:T(256)S(1)}, f32[256]{0:T(256)S(1)}, u32[]{:S(2)}, u32[]{:S(2)}) collective-permute-start(f32[256]{0:T(256)S(1)} %get-tuple-element.971), channel_id=1, source_target_pairs={{32,0},{64,32},{96,64},{128,96},{160,128},{192,160},{224,192},{256... | collective-permute-start | bytes 3080 | tf_op jit(solution)/shard_map/while/body/eval_jaxpr/ppermute | solution.py:12
  2123.8 125.3 %collective-permute-start = (f32[256]{0:T(256)S(1)}, f32[256]{0:T(256)S(1)}, u32[]{:S(2)}, u32[]{:S(2)}) collective-permute-start(f32[256]{0:T(256)S(1)} %get-tuple-element.971), channel_id=1, source_target_pairs={{32,0},{64,32},{96,64},{128,96},{160,128},{192,160},{224,192},{256... | collective-permute-start | bytes 3080 | tf_op jit(solution)/shard_map/while/body/eval_jaxpr/ppermute | solution.py:12
  2260.0 138.0 %collective-permute-start = (f32[256]{0:T(256)S(1)}, f32[256]{0:T(256)S(1)}, u32[]{:S(2)}, u32[]{:S(2)}) collective-permute-start(f32[256]{0:T(256)S(1)} %get-tuple-element.971), channel_id=1, source_target_pairs={{32,0},{64,32},{96,64},{128,96},{160,128},{192,160},{224,192},{256... | collective-permute-start | bytes 3080 | tf_op jit(solution)/shard_map/while/body/eval_jaxpr/ppermute | solution.py:12
  (49 other events, 1556.7 us)
Sparse Core Ops, SparseCore 0:
  10.6 137.3 all-reduce.2
where the time goes:
time: 2450 us; the launch traced here: 2410 us
  starting transfers between devices  1360 us (56%)
  waiting for transfers between devices  760 us (31%)
  other arithmetic  163 us (7%)
  blocking collectives  68.9 us (3%)
    ppermute x45, starting transfers between devices, passed_along(): return lax.ppermute(x, axis, pairs)  1360 us
    ppermute x45, waiting for transfers between devices, passed_along(): return lax.ppermute(x, axis, pairs)  692 us
    psum x1, blocking collectives, shards(): information, drive_vector = lax.psum((info_part, drive_part), 'sta')  68.9 us
    another operation x12, other arithmetic, spd_inverse(): lower_factor = jnp.linalg.cholesky(matrix)  68 us
    psum x1, waiting for transfers between devices, shards(): information, drive_vector = lax.psum((info_part, drive_part), 'sta')  67.6 us
  transfers between devices with their start and end apart: 46, of which 31 were waited for; matrix products, arithmetic and copies ran while one was open for 0% of the time, Pallas kernels for 0%

commit v1 on v0

v1 whole, which is shorter than its diff:
```python
import functools
import jax
import jax.numpy as jnp
from jax import lax
from jax.experimental import pallas as pl
from jax.experimental.pallas import tpu as pltpu
from jax.sharding import PartitionSpec as P

HALF = 128
TILE = 8
TOLERANCE = 1e-5
MOST_STEPS = 4000


def ray_kernel(
    spot_ref, count_ref, var_ref, basis_ref, delay_ref, station_ref, decay_ref, out_ref, weighted
):
    rays = basis_ref.shape[1]
    stations = var_ref.shape[0]
    shard = spot_ref[0]
    local = station_ref[...] - shard * stations
    variance = jnp.ones(local.shape, jnp.float32)
    for k in range(stations):
        variance = jnp.where(local == k, var_ref[k], variance)
    slot = lax.broadcasted_iota(jnp.int32, local.shape, 1)
    weight = jnp.where(slot < count_ref[0, 0], 1.0 / variance, 0.0)
    for start in range(0, rays, HALF):
        rows = slice(start, start + HALF)
        column = jnp.broadcast_to(weight[:, rows], (HALF, HALF)).T
        for lane in (0, HALF):
            lanes = slice(lane, lane + HALF)
            block = basis_ref[0, rows, lanes].astype(jnp.float32)
            weighted[rows, lanes] = (block * column).astype(jnp.bfloat16)
    scaled = weighted[...]
    information = lax.dot_general(
        scaled, basis_ref[0], (((0,), (0,)), ((), ())), preferred_element_type=jnp.float32
    )
    drive = jnp.dot(delay_ref[...], scaled, preferred_element_type=jnp.float32)
    first = information[:HALF, :HALF]
    second = information[HALF:, HALF:]
    row = lax.broadcasted_iota(jnp.int32, (HALF, HALF), 0)
    col = lax.broadcasted_iota(jnp.int32, (HALF, HALF), 1)
    diagonal = jnp.sum(jnp.where(row == col, second, 0.0), axis=0, keepdims=True)
    triangles = jnp.where(col >= row, first, second)
    groups = HALF // TILE
    shape = (groups, TILE, HALF)
    out_ref[:groups, :TILE, :] = triangles.reshape(shape)
    out_ref[groups:, :TILE, :] = information[:HALF, HALF:].reshape(shape)
    out_ref[:, TILE:, :] = jnp.zeros((2 * groups, TILE, HALF), jnp.float32)
    own = jnp.where(shard == 0, decay_ref[...], 0.0)
    extras = (drive[:, :HALF], drive[:, HALF:], diagonal, own[:, :HALF], own[:, HALF:])
    for k, extra in enumerate(extras):
        out_ref[k, TILE : TILE + 1, :] = extra


def sum_kernel(parts_ref, out_ref):
    total = jnp.sum(parts_ref[...], axis=0)
    for k in range(out_ref.shape[0]):
        out_ref[k] = total


def solve_kernel(
    spot_ref,
    mine_ref,
    other_ref,
    spread_ref,
    prior_ref,
    out_ref,
    packed,
    high,
    low,
    response,
):
    epochs, _, width = response.shape
    chips = mine_ref.shape[0]
    core = spot_ref[0]
    epoch_here = spot_ref[1]
    row = lax.broadcasted_iota(jnp.int32, (HALF, HALF), 0)
    col = lax.broadcasted_iota(jnp.int32, (HALF, HALF), 1)

    def unpack(e, carry):
        place = pl.multiple_of(e * TILE, TILE)
        for j in range(chips):
            ours = pl.multiple_of(2 * j * TILE + core * TILE, TILE)
            theirs = pl.multiple_of(2 * j * TILE + (1 - core) * TILE, TILE)
            packed[pl.ds(ours, TILE), :] = mine_ref[j, pl.ds(place, TILE), :]
            packed[pl.ds(theirs, TILE), :] = other_ref[j, pl.ds(place, TILE), :]
        triangles = packed[:HALF, :]
        corner = packed[HALF:, :]
        turned = triangles.T
        on_diagonal = row == col
        own = jnp.sum(jnp.where(on_diagonal, triangles, 0.0), axis=0, keepdims=True)
        first = jnp.where(on_diagonal, 0.0, jnp.where(col > row, triangles, turned))
        second = jnp.where(on_diagonal, 0.0, jnp.where(col < row, triangles, turned))
        base = pl.multiple_of(e * width, width)
        for r, c, block in ((0, 0, first), (0, 1, corner), (1, 0, corner.T), (1, 1, second)):
            rows = pl.ds(base + r * HALF, HALF)
            lanes = slice(c * HALF, c * HALF + HALF)
            upper = block.astype(jnp.bfloat16)
            high[rows, lanes] = upper
            low[rows, lanes] = (block - upper.astype(jnp.float32)).astype(jnp.bfloat16)
        return jnp.where(epoch_rows == e, own, carry)

    epoch_rows = lax.broadcasted_iota(jnp.int32, (epochs, HALF), 0)
    corner_diagonal = lax.fori_loop(0, epochs, unpack, jnp.zeros((epochs, HALF), jnp.float32))

    def extra(k):
        rows = slice(epochs * TILE, epochs * TILE + epochs)
        return jnp.where(core == k % 2, mine_ref[k // 2, rows, :], other_ref[k // 2, rows, :])

    drive = jnp.concatenate([extra(0), extra(1)], axis=1)
    decay = jnp.concatenate([extra(3), extra(4)], axis=1)
    diagonal = jnp.concatenate([corner_diagonal, extra(2)], axis=1)
    inverse_noise = 1.0 / ((1.0 - decay * decay) * spread_ref[...])
    index = lax.broadcasted_iota(jnp.int32, (epochs, width), 0)
    pull = decay * inverse_noise
    link_back = jnp.where(index == 0, 0.0, pull)
    link = jnp.where(index == epochs - 1, 0.0, pltpu.roll(pull, epochs - 1, 0))
    carried = jnp.where(index == epochs - 1, 0.0, pltpu.roll(decay * pull, epochs - 1, 0))
    middle = inverse_noise + carried + diagonal
    right = drive + jnp.where(index == 0, pull * prior_ref[...], 0.0)

    at = lambda x, e: x[e : e + 1, :]
    ahead = [at(middle, 0)]
    up = []
    for e in range(epochs - 1):
        up.append(at(link, e) / ahead[e])
        ahead.append(at(middle, e + 1) - at(link, e) * up[e])
    behind = at(middle, epochs - 1)
    down = [None] * epochs
    centre = [None] * epochs
    centre[epochs - 1] = 1.0 / ahead[epochs - 1]
    for e in reversed(range(epochs - 1)):
        down[e] = at(link, e) / behind
        reduced = at(link, e) * down[e]
        behind = at(middle, e) - reduced
        centre[e] = 1.0 / (ahead[e] - reduced)
    below = jnp.zeros((epochs, width), jnp.float32)
    for e in range(epochs):
        if e:
            below = below * down[e - 1]
        below = jnp.where(index == e, centre[e], below)
        response[e] = below
    above = jnp.where(index == epochs - 1, centre[epochs - 1], 0.0)
    for e in reversed(range(epochs - 1)):
        above = above * up[e]
        response[e] = response[e] + above
        above = jnp.where(index == e, centre[e], above)

    def precondition(r):
        total = at(r, 0) * response[0]
        for e in range(1, epochs):
            total = total + at(r, e) * response[e]
        return total

    def apply(p):
        blocks = []
        for e in range(epochs):
            kept = jnp.where(index == e, p, 0.0)
            upper = kept.astype(jnp.bfloat16)
            rest = (kept - upper.astype(jnp.float32)).astype(jnp.bfloat16)
            blocks.append(jnp.concatenate([upper, rest], axis=0))
        left = jnp.concatenate(blocks, axis=1)
        by_high = jnp.dot(left, high[...], preferred_element_type=jnp.float32)
        by_low = jnp.dot(left[:epochs], low[...], preferred_element_type=jnp.float32)
        near = (
            middle * p
            - link * pltpu.roll(p, epochs - 1, 0)
            - link_back * pltpu.roll(p, 1, 0)
        )
        return near + (by_high[:epochs] + by_high[epochs:] + by_low)

    def inner(a, b):
        return jnp.sum(jnp.sum(a * b, axis=0, keepdims=True), axis=1, keepdims=True)

    start = precondition(right)
    size = inner(right, start)
    bound = size[0, 0] * (TOLERANCE * TOLERANCE)

    def unfinished(state):
        return jnp.logical_and(state[0] < MOST_STEPS, state[5][0, 0] > bound)

    def step(state):
        count, x, r, p, _, size = state
        image = apply(p)
        energy = inner(p, image)
        length = jnp.where(energy > 0.0, size / energy, 0.0)
        x = x + length * p
        r = r - length * image
        z = precondition(r)
        fresh = inner(r, z)
        ratio = jnp.where(size > 0.0, fresh / size, 0.0)
        p = z + ratio * p
        return (count + 1, x, r, p, z, fresh)

    zero = jnp.zeros((epochs, width), jnp.float32)
    state = lax.while_loop(unfinished, step, (0, zero, right, start, zero, size))
    solved = state[1]
    out_ref[...] = jnp.sum(jnp.where(index == epoch_here, solved, 0.0), axis=0, keepdims=True)


VMEM = pl.BlockSpec(memory_space=pltpu.VMEM)
SMEM = pl.BlockSpec(memory_space=pltpu.SMEM)


def solve(spot, mine, other, spread, prior, epochs, width):
    return pl.pallas_call(
        solve_kernel,
        out_shape=jax.ShapeDtypeStruct((1, width), jnp.float32),
        in_specs=[SMEM, VMEM, VMEM, VMEM, VMEM],
        out_specs=VMEM,
        scratch_shapes=[
            pltpu.VMEM((width, HALF), jnp.float32),
            pltpu.VMEM((epochs * width, width), jnp.bfloat16),
            pltpu.VMEM((epochs * width, width), jnp.bfloat16),
            pltpu.VMEM((epochs, epochs, width), jnp.float32),
        ],
        compiler_params=pltpu.CompilerParams(vmem_limit_bytes=48 * 2**20),
    )(spot, mine, other, spread, prior)


def shards(
    ray_basis, delays, ray_station, ray_count, station_var, decay_factor, mode_variance, prior_mean
):
    rays, width = ray_basis.shape[1:]
    epochs = lax.axis_size("tm")
    parts = lax.axis_size("sta")
    chips = parts // 2
    shard = lax.axis_index("sta")
    core = lax.rem(shard, 2)
    slab = 2 * TILE
    share = pl.pallas_call(
        ray_kernel,
        out_shape=jax.ShapeDtypeStruct((parts, slab, HALF), jnp.float32),
        in_specs=[SMEM, SMEM, SMEM, VMEM, VMEM, VMEM, VMEM],
        out_specs=VMEM,
        scratch_shapes=[pltpu.VMEM((rays, width), jnp.bfloat16)],
        compiler_params=pltpu.CompilerParams(vmem_limit_bytes=32 * 2**20),
    )(shard[None], ray_count, station_var, ray_basis, delays, ray_station, decay_factor)
    spread = lax.all_to_all(share, "sta", split_axis=0, concat_axis=0, tiled=True)
    copies = pl.pallas_call(
        sum_kernel,
        out_shape=jax.ShapeDtypeStruct((epochs, slab, HALF), jnp.float32),
        in_specs=[VMEM],
        out_specs=VMEM,
    )(spread)
    rows = lax.all_to_all(copies, "tm", split_axis=0, concat_axis=0, tiled=True)
    ours = jnp.concatenate([rows[:, :TILE].reshape(epochs * TILE, HALF), rows[:, TILE]], axis=0)
    same_core = [[2 * j + c for j in range(chips)] for c in range(2)]
    mine = lax.all_to_all(
        jnp.broadcast_to(ours[None], (chips,) + ours.shape),
        "sta",
        split_axis=0,
        concat_axis=0,
        tiled=True,
        axis_index_groups=same_core,
    )
    other = lax.ppermute(mine, "sta", [(i, i + 1 - 2 * (i % 2)) for i in range(parts)])
    spot = jnp.stack([core, lax.axis_index("tm")])
    return solve(spot, mine, other, mode_variance[None], prior_mean[None], epochs, width)


def solution(mesh):
    placed = (
        P("tm", "sta", None),
        P("tm", "sta"),
        P("tm", "sta"),
        P("tm", "sta"),
        P("sta"),
        P("tm", None),
        P(),
        P(),
    )
    return jax.shard_map(
        shards, mesh=mesh, in_specs=placed, out_specs=P("tm", None), check_vma=False
    )
```

time: 2450 us -> 96 us (0.04); the launches traced: 2410 us -> 95.5 us
  starting transfers between devices: 1360 us -> 5.77 us
  waiting for transfers between devices: 760 us -> 2.37 us
  other arithmetic: 163 us -> 0.08 us
    ppermute x45 -> x1, starting transfers between devices: 1360 us -> 5.77 us  [shards(): lax.ppermute(mine, 'sta', [(i, i + 1 - 2 * (i % 2)) for i in range(parts)])]
    ppermute x45 -> x1, waiting for transfers between devices: 692 us -> 2.37 us  [shards(): lax.ppermute(mine, 'sta', [(i, i + 1 - 2 * (i % 2)) for i in range(parts)])]
    another operation x31 -> x1, other arithmetic: 163 us -> 0.08 us  [shards(): spot = jnp.stack([core, lax.axis_index('tm')])]
    psum x1 -> x0, blocking collectives: 68.9 us -> none  [shards(): information, drive_vector = lax.psum((info_part, drive_part), 'sta')]
    psum x1 -> x0, waiting for transfers between devices: 67.6 us -> none  [shards(): information, drive_vector = lax.psum((info_part, drive_part), 'sta')]
    all_to_all x0 -> x3, blocking collectives: none -> 63.5 us  [the longest x1 25.3 us: shards(): rows = lax.all_to_all(copies, 'tm', split_axis=0, concat_axis=0, tiled=True)]
  transfers between devices with their start and end apart: 46 -> 1, of which waited for: 31 -> 1; matrix products, arithmetic and copies ran while one was open for 0% -> 0% of each run, Pallas kernels for 0% -> 0%
where the time goes in v1:
time: 96 us; the launch traced here: 95.5 us
  blocking collectives  63.5 us (66%)
  Pallas kernels  19.2 us (20%)
  starting transfers between devices  5.77 us (6%)
  local copies, waits for them, and re-layouts  3.84 us (4%)
  waiting for transfers between devices  2.37 us (2%)
    all_to_all x1, blocking collectives, shards(): rows = lax.all_to_all(copies, 'tm', split_axis=0, concat_axis=0, tiled=True)  25.3 us
    all_to_all x1, blocking collectives, shards(): lax.all_to_all(share, 'sta', split_axis=0, concat_axis=0, tiled=True)  19.2 us
    all_to_all x1, blocking collectives, shards(): lax.all_to_all(jnp.broadcast_to(ours[None], (chips,) + ours.shape), 'sta'...  19 us
    pallas_call x1, Pallas kernels, solve(): pl.pallas_call(solve_kernel, out_shape=jax.ShapeDtypeStruct((1, width), j...  16.4 us
    ppermute x1, starting transfers between devices, shards(): lax.ppermute(mine, 'sta', [(i, i + 1 - 2 * (i % 2)) for i in range(parts)])  5.77 us
    unnamed x14, local copies, waits for them, and re-layouts  3.75 us
    ppermute x1, waiting for transfers between devices, shards(): lax.ppermute(mine, 'sta', [(i, i + 1 - 2 * (i % 2)) for i in range(parts)])  2.37 us
  transfers between devices with their start and end apart: 1, of which 1 were waited for; matrix products, arithmetic and copies ran while one was open for 0% of the time, Pallas kernels for 0%

profile of v1, /device:TPU:1, one launch (start us, length us, event | category | flops | bytes accessed | tf_op | source)
XLA Modules:
  0.0 95.5 jit_solution(16261470655099529316)
XLA Ops:
  0.7 0.0 copy-start
  0.7 1.0 %copy-done = bf16[1,1024,256]{2,1,0:T(8,128)(2,1)S(1)} copy-done((bf16[1,1024,256]{2,1,0:T(8,128)(2,1)S(1)}, bf16[1,1024,256]{2,1,0:T(8,128)(2,1)}, u32[]{:S(2)}) %copy-start) | copy-done | bytes 524312
  1.7 0.0 copy-start.1
  1.7 0.7 copy-done.1
  2.4 0.0 copy-start.2
  2.4 0.7 copy-done.2
  3.1 0.0 copy-start.3
  3.1 0.7 copy-done.3
  3.7 0.0 copy-start.6
  3.8 0.7 copy-done.6
  4.4 1.2 %shard_map.82 = f32[32,16,128]{2,1,0:T(8,128)S(1)} custom-call(s32[1]{0:T(128)} %bitcast.2.spot_ref, s32[1,1]{1,0:T(1,128)S(6)} %copy.9.count_ref, f32[16]{0:T(128)S(1)} %copy-done.6, bf16[1,1024,256]{2,1,0:T(8,128)(2,1)S(1)} %copy-done, bf16[1,1024]{1,0:T(2,128)(2,1)S(1)} %copy-done.1, s32[1,1024]{1,0:T(1,128)S(1)} %copy-done.2, f32[1,256]{1,0:T(1,128)S(1)} %copy-done.3), custom_call_target="tpu_custom_call" | custom-call | tf_op jit(solution)/shard_map/pallas_call | solution.py:232
  5.6 19.2 %all_to_all.15.parts_ref = f32[32,16,128]{2,1,0:T(8,128)} all-to-all(f32[32,16,128]{2,1,0:T(8,128)S(1)} %shard_map.82), channel_id=1, replica_groups=mesh['tm'=16,'sta'=32] {'sta'}, dimensions={0} | all-to-all | bytes 524288 | tf_op jit(solution)/shard_map/all_to_all | solution.py:240
  24.8 1.6 %shard_map.83 = f32[16,16,128]{2,1,0:T(8,128)} custom-call(f32[32,16,128]{2,1,0:T(8,128)} %all_to_all.15.parts_ref), custom_call_target="tpu_custom_call" | custom-call | tf_op jit(solution)/shard_map/pallas_call | solution.py:241
  26.4 25.3 %all_to_all.16 = f32[16,16,128]{2,1,0:T(8,128)S(1)} all-to-all(f32[16,16,128]{2,1,0:T(8,128)} %shard_map.83), channel_id=1, replica_groups=mesh['tm'=16,'sta'=32] {'tm'}, dimensions={0} | all-to-all | bytes 262144 | tf_op jit(solution)/shard_map/all_to_all | solution.py:247
  51.7 0.1 broadcast_in_dim.16
  51.8 0.0 copy-start.4
  51.8 0.0 copy-start.5
  51.9 19.0 %all_to_all.17.mine_ref = f32[16,144,128]{2,1,0:T(8,128)S(1)} all-to-all(f32[16,144,128]{2,1,0:T(8,128)S(1)} %broadcast_in_dim.16), channel_id=1, replica_groups={{0,2,4,6,8,10,12,14,16,18,20,22,24,26,28,30},{1,3,5,7,9,11,13,15,17,19,..., dimensions={0} | all-to-all | bytes 2359296 | tf_op jit(solution)/shard_map/all_to_all | solution.py:250
  70.8 5.8 %collective-permute-start = (f32[16,144,128]{2,1,0:T(8,128)S(1)}, f32[16,144,128]{2,1,0:T(8,128)S(1)}, u32[]{:S(2)}, u32[]{:S(2)}) collective-permute-start(f32[16,144,128]{2,1,0:T(8,128)S(1)} %all_to_all.17.mine_ref), channel_id=1, source_target_pairs={{0,1},{1,0},{2,3},{3,2},{4,5},{5,4},{6,7},{7,6},{8,9},{9,8},{10,11... | collective-permute-start | bytes 3538952 | tf_op jit(solution)/shard_map/ppermute | solution.py:258
  76.6 0.1 pad_add_fusion.spot_ref
  76.7 2.4 %collective-permute-done.other_ref = f32[16,144,128]{2,1,0:T(8,128)S(1)} collective-permute-done((f32[16,144,128]{2,1,0:T(8,128)S(1)}, f32[16,144,128]{2,1,0:T(8,128)S(1)}, u32[]{:S(2)}, u32[]{:S(2)}) %collective-permute-start) | collective-permute-done | bytes 1179680 | tf_op jit(solution)/shard_map/ppermute | solution.py:258
  79.1 0.0 copy-done.4
  79.1 0.0 copy-done.5
  79.1 16.4 %shard_map.84 = f32[1,256]{1,0:T(1,128)} custom-call(s32[2]{0:T(128)S(1)} %pad_add_fusion.spot_ref, f32[16,144,128]{2,1,0:T(8,128)S(1)} %all_to_all.17.mine_ref, f32[16,144,128]{2,1,0:T(8,128)S(1)} %collective-permute-done.other_ref, f32[1,256]{1,0:T(1,128)S(1)} %bitcast.8, f32[1,256]{1,0:T(1,128)S(1)} %bitcast.9), custom_call_target="tpu_custom_call" | custom-call | tf_op jit(solution)/shard_map/pallas_call | solution.py:207
  (3 shorter events, 0.0 us)
Async XLA Ops:
  0.7 1.0 %copy-start = (bf16[1,1024,256]{2,1,0:T(8,128)(2,1)S(1)}, bf16[1,1024,256]{2,1,0:T(8,128)(2,1)}, u32[]{:S(2)}) copy-start(bf16[1,1024,256]{2,1,0:T(8,128)(2,1)} %basis_ref.1) | copy-start | bytes 1572868
  1.7 0.7 copy-start.1
  2.4 0.7 copy-start.2
  3.1 0.7 copy-start.3
  3.7 0.7 copy-start.6
  51.8 27.2 %copy-start.4 = (f32[256]{0:T(256)S(1)}, f32[256]{0:T(256)}, u32[]{:S(2)}) copy-start(f32[256]{0:T(256)} %param.14) | copy-start | bytes 3076
  51.8 27.2 %copy-start.5 = (f32[256]{0:T(256)S(1)}, f32[256]{0:T(256)}, u32[]{:S(2)}) copy-start(f32[256]{0:T(256)} %param.15) | copy-start | bytes 3076
  70.8 8.2 %collective-permute-start = (f32[16,144,128]{2,1,0:T(8,128)S(1)}, f32[16,144,128]{2,1,0:T(8,128)S(1)}, u32[]{:S(2)}, u32[]{:S(2)}) collective-permute-start(f32[16,144,128]{2,1,0:T(8,128)S(1)} %all_to_all.17.mine_ref), channel_id=1, source_target_pairs={{0,1},{1,0},{2,3},{3,2},{4,5},{5,4},{6,7},{7,6},{8,9},{9,8},{10,11... | collective-permute-start | bytes 3538952 | tf_op jit(solution)/shard_map/ppermute | solution.py:258

commit v2 on v1

--- a/solution.py
+++ b/solution.py
@@ -1,4 +1,3 @@
-import functools
 import jax
 import jax.numpy as jnp
 from jax import lax
@@ -8,32 +7,66 @@
 
 HALF = 128
 TILE = 8
+SLAB = TILE + 1
 TOLERANCE = 1e-5
 MOST_STEPS = 4000
 
 
 def ray_kernel(
-    spot_ref, count_ref, var_ref, basis_ref, delay_ref, station_ref, decay_ref, out_ref, weighted
+    count_hbm,
+    var_hbm,
+    basis_hbm,
+    delay_hbm,
+    station_hbm,
+    decay_hbm,
+    out_ref,
+    count_ref,
+    var_ref,
+    basis_ref,
+    delay_ref,
+    station_ref,
+    decay_ref,
+    weighted,
+    arrived,
 ):
-    rays = basis_ref.shape[1]
+    rays = basis_ref.shape[0]
     stations = var_ref.shape[0]
-    shard = spot_ref[0]
+    small = [
+        pltpu.make_async_copy(source, target, arrived.at[k])
+        for k, (source, target) in enumerate(
+            (
+                (station_hbm, station_ref),
+                (var_hbm, var_ref),
+                (count_hbm, count_ref),
+                (delay_hbm, delay_ref),
+                (decay_hbm, decay_ref),
+            )
+        )
+    ]
+    whole = pltpu.make_async_copy(basis_hbm.at[0], basis_ref, arrived.at[len(small)])
+    for copy in small:
+        copy.start()
+    whole.start()
+    shard = lax.axis_index("sta")
+    for copy in small:
+        copy.wait()
     local = station_ref[...] - shard * stations
     variance = jnp.ones(local.shape, jnp.float32)
     for k in range(stations):
         variance = jnp.where(local == k, var_ref[k], variance)
     slot = lax.broadcasted_iota(jnp.int32, local.shape, 1)
     weight = jnp.where(slot < count_ref[0, 0], 1.0 / variance, 0.0)
+    whole.wait()
     for start in range(0, rays, HALF):
         rows = slice(start, start + HALF)
         column = jnp.broadcast_to(weight[:, rows], (HALF, HALF)).T
         for lane in (0, HALF):
             lanes = slice(lane, lane + HALF)
-            block = basis_ref[0, rows, lanes].astype(jnp.float32)
+            block = basis_ref[rows, lanes].astype(jnp.float32)
             weighted[rows, lanes] = (block * column).astype(jnp.bfloat16)
     scaled = weighted[...]
     information = lax.dot_general(
-        scaled, basis_ref[0], (((0,), (0,)), ((), ())), preferred_element_type=jnp.float32
+        scaled, basis_ref[...], (((0,), (0,)), ((), ())), preferred_element_type=jnp.float32
     )
     drive = jnp.dot(delay_ref[...], scaled, preferred_element_type=jnp.float32)
     first = information[:HALF, :HALF]
@@ -42,25 +75,42 @@
     col = lax.broadcasted_iota(jnp.int32, (HALF, HALF), 1)
     diagonal = jnp.sum(jnp.where(row == col, second, 0.0), axis=0, keepdims=True)
     triangles = jnp.where(col >= row, first, second)
-    groups = HALF // TILE
-    shape = (groups, TILE, HALF)
-    out_ref[:groups, :TILE, :] = triangles.reshape(shape)
-    out_ref[groups:, :TILE, :] = information[:HALF, HALF:].reshape(shape)
-    out_ref[:, TILE:, :] = jnp.zeros((2 * groups, TILE, HALF), jnp.float32)
+    corner = information[:HALF, HALF:]
     own = jnp.where(shard == 0, decay_ref[...], 0.0)
-    extras = (drive[:, :HALF], drive[:, HALF:], diagonal, own[:, :HALF], own[:, HALF:])
-    for k, extra in enumerate(extras):
-        out_ref[k, TILE : TILE + 1, :] = extra
+    extras = [drive[:, :HALF], drive[:, HALF:], diagonal, own[:, :HALF], own[:, HALF:]]
+    blank = jnp.zeros((1, HALF), jnp.float32)
+    for j in range(HALF // TILE):
+        extra = extras[j] if j < len(extras) else blank
+        for c, block in ((0, triangles), (1, corner)):
+            base = (2 * j + c) * SLAB
+            out_ref[base : base + TILE, 0, :] = block[j * TILE : j * TILE + TILE, :]
+            out_ref[base + TILE, :, :] = extra
 
 
 def sum_kernel(parts_ref, out_ref):
-    total = jnp.sum(parts_ref[...], axis=0)
-    for k in range(out_ref.shape[0]):
-        out_ref[k] = total
+    total = parts_ref[0:TILE, 0, :]
+    extra = parts_ref[TILE, :, :]
+    for k in range(1, parts_ref.shape[0] // SLAB):
+        base = k * SLAB
+        total = total + parts_ref[base : base + TILE, 0, :]
+        extra = extra + parts_ref[base + TILE, :, :]
+    for k in range(out_ref.shape[0] // SLAB):
+        base = k * SLAB
+        out_ref[base : base + TILE, 0, :] = total
+        out_ref[base + TILE, :, :] = extra
+
+
+def copy_kernel(rows_ref, out_ref):
+    epochs = rows_ref.shape[0] // SLAB
+    for k in range(epochs):
+        tile = rows_ref[k * SLAB : k * SLAB + TILE, 0, :]
+        extra = rows_ref[k * SLAB + TILE, :, :]
+        for j in range(out_ref.shape[0]):
+            out_ref[j, k * TILE : k * TILE + TILE, :] = tile
+            out_ref[j, epochs * TILE + k : epochs * TILE + k + 1, :] = extra
 
 
 def solve_kernel(
-    spot_ref,
     mine_ref,
     other_ref,
     spread_ref,
@@ -73,16 +123,16 @@
 ):
     epochs, _, width = response.shape
     chips = mine_ref.shape[0]
-    core = spot_ref[0]
-    epoch_here = spot_ref[1]
+    core = lax.rem(lax.axis_index("sta"), 2)
+    epoch_here = lax.axis_index("tm")
     row = lax.broadcasted_iota(jnp.int32, (HALF, HALF), 0)
     col = lax.broadcasted_iota(jnp.int32, (HALF, HALF), 1)
 
     def unpack(e, carry):
         place = pl.multiple_of(e * TILE, TILE)
         for j in range(chips):
-            ours = pl.multiple_of(2 * j * TILE + core * TILE, TILE)
-            theirs = pl.multiple_of(2 * j * TILE + (1 - core) * TILE, TILE)
+            ours = pl.multiple_of(core * HALF + j * TILE, TILE)
+            theirs = pl.multiple_of((1 - core) * HALF + j * TILE, TILE)
             packed[pl.ds(ours, TILE), :] = mine_ref[j, pl.ds(place, TILE), :]
             packed[pl.ds(theirs, TILE), :] = other_ref[j, pl.ds(place, TILE), :]
         triangles = packed[:HALF, :]
@@ -105,8 +155,7 @@
     corner_diagonal = lax.fori_loop(0, epochs, unpack, jnp.zeros((epochs, HALF), jnp.float32))
 
     def extra(k):
-        rows = slice(epochs * TILE, epochs * TILE + epochs)
-        return jnp.where(core == k % 2, mine_ref[k // 2, rows, :], other_ref[k // 2, rows, :])
+        return mine_ref[k, epochs * TILE : epochs * TILE + epochs, :]
 
     drive = jnp.concatenate([extra(0), extra(1)], axis=1)
     decay = jnp.concatenate([extra(3), extra(4)], axis=1)
@@ -178,86 +227,104 @@
     bound = size[0, 0] * (TOLERANCE * TOLERANCE)
 
     def unfinished(state):
-        return jnp.logical_and(state[0] < MOST_STEPS, state[5][0, 0] > bound)
+        return jnp.logical_and(state[0] < MOST_STEPS, state[6][0, 0] > bound)
 
     def step(state):
-        count, x, r, p, _, size = state
-        image = apply(p)
-        energy = inner(p, image)
+        count, x, r, z, p, path, size, before, length = state
+        image = apply(z)
+        energy = inner(z, image)
+        ratio = jnp.where(before > 0.0, size / before, 0.0)
+        past = jnp.where(length > 0.0, ratio * size / length, 0.0)
+        energy = energy - past
         length = jnp.where(energy > 0.0, size / energy, 0.0)
+        p = z + ratio * p
+        path = image + ratio * path
         x = x + length * p
-        r = r - length * image
+        r = r - length * path
         z = precondition(r)
-        fresh = inner(r, z)
-        ratio = jnp.where(size > 0.0, fresh / size, 0.0)
-        p = z + ratio * p
-        return (count + 1, x, r, p, z, fresh)
+        return (count + 1, x, r, z, p, path, inner(r, z), size, length)
 
     zero = jnp.zeros((epochs, width), jnp.float32)
-    state = lax.while_loop(unfinished, step, (0, zero, right, start, zero, size))
-    solved = state[1]
+    none = jnp.zeros((1, 1), jnp.float32)
+    state = (0, zero, right, start, zero, zero, size, none, none)
+    solved = lax.while_loop(unfinished, step, state)[1]
     out_ref[...] = jnp.sum(jnp.where(index == epoch_here, solved, 0.0), axis=0, keepdims=True)
 
 
 VMEM = pl.BlockSpec(memory_space=pltpu.VMEM)
-SMEM = pl.BlockSpec(memory_space=pltpu.SMEM)
-
-
-def solve(spot, mine, other, spread, prior, epochs, width):
+HBM = pl.BlockSpec(memory_space=pltpu.HBM)
+MIB = 2**20
+
+
+def call(kernel, shape, specs, scratch, vmem, *operands):
     return pl.pallas_call(
-        solve_kernel,
-        out_shape=jax.ShapeDtypeStruct((1, width), jnp.float32),
-        in_specs=[SMEM, VMEM, VMEM, VMEM, VMEM],
+        kernel,
+        out_shape=jax.ShapeDtypeStruct(shape, jnp.float32),
+        in_specs=specs,
         out_specs=VMEM,
-        scratch_shapes=[
-            pltpu.VMEM((width, HALF), jnp.float32),
-            pltpu.VMEM((epochs * width, width), jnp.bfloat16),
-            pltpu.VMEM((epochs * width, width), jnp.bfloat16),
-            pltpu.VMEM((epochs, epochs, width), jnp.float32),
-        ],
-        compiler_params=pltpu.CompilerParams(vmem_limit_bytes=48 * 2**20),
-    )(spot, mine, other, spread, prior)
+        scratch_shapes=scratch,
+        compiler_params=pltpu.CompilerParams(vmem_limit_bytes=vmem * MIB),
+    )(*operands)
+
+
+def solve(mine, other, spread, prior, epochs, width):
+    scratch = [
+        pltpu.VMEM((width, HALF), jnp.float32),
+        pltpu.VMEM((epochs * width, width), jnp.bfloat16),
+        pltpu.VMEM((epochs * width, width), jnp.bfloat16),
+        pltpu.VMEM((epochs, epochs, width), jnp.float32),
+    ]
+    return call(solve_kernel, (1, width), [VMEM] * 4, scratch, 24, mine, other, spread, prior)
+
+
+def exchange(x, axis, groups=None):
+    return lax.all_to_all(
+        x, axis, split_axis=0, concat_axis=0, tiled=True, axis_index_groups=groups
+    )
 
 
 def shards(
     ray_basis, delays, ray_station, ray_count, station_var, decay_factor, mode_variance, prior_mean
 ):
     rays, width = ray_basis.shape[1:]
+    stations = station_var.shape[0]
     epochs = lax.axis_size("tm")
     parts = lax.axis_size("sta")
     chips = parts // 2
-    shard = lax.axis_index("sta")
-    core = lax.rem(shard, 2)
-    slab = 2 * TILE
-    share = pl.pallas_call(
+    scratch = [
+        pltpu.SMEM((1, 1), jnp.int32),
+        pltpu.SMEM((stations,), jnp.float32),
+        pltpu.VMEM((rays, width), jnp.bfloat16),
+        pltpu.VMEM((1, rays), jnp.bfloat16),
+        pltpu.VMEM((1, rays), jnp.int32),
+        pltpu.VMEM((1, width), jnp.float32),
+        pltpu.VMEM((rays, width), jnp.bfloat16),
+        pltpu.SemaphoreType.DMA((6,)),
+    ]
+    share = call(
         ray_kernel,
-        out_shape=jax.ShapeDtypeStruct((parts, slab, HALF), jnp.float32),
-        in_specs=[SMEM, SMEM, SMEM, VMEM, VMEM, VMEM, VMEM],
-        out_specs=VMEM,
-        scratch_shapes=[pltpu.VMEM((rays, width), jnp.bfloat16)],
-        compiler_params=pltpu.CompilerParams(vmem_limit_bytes=32 * 2**20),
-    )(shard[None], ray_count, station_var, ray_basis, delays, ray_station, decay_factor)
-    spread = lax.all_to_all(share, "sta", split_axis=0, concat_axis=0, tiled=True)
-    copies = pl.pallas_call(
-        sum_kernel,
-        out_shape=jax.ShapeDtypeStruct((epochs, slab, HALF), jnp.float32),
-        in_specs=[VMEM],
-        out_specs=VMEM,
-    )(spread)
-    rows = lax.all_to_all(copies, "tm", split_axis=0, concat_axis=0, tiled=True)
-    ours = jnp.concatenate([rows[:, :TILE].reshape(epochs * TILE, HALF), rows[:, TILE]], axis=0)
+        (parts * SLAB, 1, HALF),
+        [HBM] * 6,
+        scratch,
+        16,
+        ray_count,
+        station_var,
+        ray_basis,
+        delays,
+        ray_station,
+        decay_factor,
+    )
+    summed = call(
+        sum_kernel, (epochs * SLAB, 1, HALF), [VMEM], [], 4, exchange(share, "sta")
+    )
+    ours = call(
+        copy_kernel, (chips, epochs * SLAB, HALF), [VMEM], [], 4, exchange(summed, "tm")
+    )
     same_core = [[2 * j + c for j in range(chips)] for c in range(2)]
-    mine = lax.all_to_all(
-        jnp.broadcast_to(ours[None], (chips,) + ours.shape),
-        "sta",
-        split_axis=0,
-        concat_axis=0,
-        tiled=True,
-        axis_index_groups=same_core,
-    )
+    ours = ours.reshape(chips * epochs * SLAB, HALF)
+    mine = exchange(ours, "sta", same_core).reshape(chips, epochs * SLAB, HALF)
     other = lax.ppermute(mine, "sta", [(i, i + 1 - 2 * (i % 2)) for i in range(parts)])
-    spot = jnp.stack([core, lax.axis_index("tm")])
-    return solve(spot, mine, other, mode_variance[None], prior_mean[None], epochs, width)
+    return solve(mine, other, mode_variance[None], prior_mean[None], epochs, width)
 
 
 def solution(mesh):

time: 96 us -> 95.7 us (level)
  Pallas kernels: 19.2 us -> 21.1 us
  blocking collectives: 63.5 us -> 62.4 us
    pallas_call x3 -> x4, Pallas kernels: 19.2 us -> 21.1 us  [call(): pl.pallas_call(kernel, out_shape=jax.ShapeDtypeStruct(shape, jnp.float32)...]
    all_to_all x3, blocking collectives: 63.5 us -> 62.4 us  [exchange(): lax.all_to_all(x, axis, split_axis=0, concat_axis=0, tiled=True, axis_ind...]
where the time goes in v2:
time: 95.7 us; the launch traced here: 95.3 us
  blocking collectives  62.4 us (65%)
  Pallas kernels  21.1 us (22%)
  starting transfers between devices  4.94 us (5%)
  local copies, waits for them, and re-layouts  3.75 us (4%)
  waiting for transfers between devices  2.45 us (3%)
    all_to_all x3, blocking collectives, exchange(): lax.all_to_all(x, axis, split_axis=0, concat_axis=0, tiled=True, axis_ind...  62.4 us
    pallas_call x4, Pallas kernels, call(): pl.pallas_call(kernel, out_shape=jax.ShapeDtypeStruct(shape, jnp.float32)...  21.1 us
    ppermute x1, starting transfers between devices, shards(): lax.ppermute(mine, 'sta', [(i, i + 1 - 2 * (i % 2)) for i in range(parts)])  4.94 us
    unnamed x14, local copies, waits for them, and re-layouts  3.75 us
    ppermute x1, waiting for transfers between devices, shards(): lax.ppermute(mine, 'sta', [(i, i + 1 - 2 * (i % 2)) for i in range(parts)])  2.45 us
  transfers between devices with their start and end apart: 1, of which 1 were waited for; matrix products, arithmetic and copies ran while one was open for 0% of the time, Pallas kernels for 0%

profile of v2, /device:TPU:1, one launch (start us, length us, event | category | flops | bytes accessed | tf_op | source)
XLA Modules:
  0.0 95.3 jit_solution(11338066308975538073)
XLA Ops:
  0.7 0.0 copy-start
  0.7 1.0 %copy-done = bf16[1,1024,256]{2,1,0:T(8,128)(2,1)S(1)} copy-done((bf16[1,1024,256]{2,1,0:T(8,128)(2,1)S(1)}, bf16[1,1024,256]{2,1,0:T(8,128)(2,1)}, u32[]{:S(2)}) %copy-start) | copy-done | bytes 524312
  1.7 0.0 copy-start.1
  1.7 0.7 copy-done.1
  2.4 0.0 copy-start.2
  2.4 0.7 copy-done.2
  3.1 0.0 copy-start.5
  3.1 0.7 copy-done.5
  3.7 0.0 copy-start.6
  3.8 0.7 copy-done.6
  4.4 1.3 %shard_map.82 = f32[288,1,128]{2,1,0:T(1,128)S(1)} custom-call(s32[1,1]{1,0:T(1,128)S(6)} %copy.9.count_hbm, f32[16]{0:T(128)S(1)} %copy-done.6, bf16[1,1024,256]{2,1,0:T(8,128)(2,1)S(1)} %copy-done, bf16[1,1024]{1,0:T(2,128)(2,1)S(1)} %copy-done.1, s32[1,1024]{1,0:T(1,128)S(1)} %copy-done.2, f32[1,256]{1,0:T(1,128)S(1)} %copy-done.5), custom_call_target="tpu_custom_call" | custom-call | tf_op jit(solution)/shard_map/pallas_call | solution.py:260
  5.7 17.4 %all_to_all.16.parts_ref = f32[288,1,128]{2,1,0:T(1,128)S(1)} all-to-all(f32[288,1,128]{2,1,0:T(1,128)S(1)} %shard_map.82), channel_id=1, replica_groups=mesh['tm'=16,'sta'=32] {'sta'}, dimensions={0} | all-to-all | bytes 294912 | tf_op jit(solution)/shard_map/all_to_all | solution.py:281
  23.1 0.1 shard_map.83
  23.2 25.2 %all_to_all.17.rows_ref = f32[144,1,128]{2,1,0:T(1,128)S(1)} all-to-all(f32[144,1,128]{2,1,0:T(1,128)S(1)} %shard_map.83), channel_id=1, replica_groups=mesh['tm'=16,'sta'=32] {'tm'}, dimensions={0} | all-to-all | bytes 147456 | tf_op jit(solution)/shard_map/all_to_all | solution.py:281
  48.4 0.1 shard_map.84
  48.5 0.0 copy-start.3
  48.6 0.0 copy-start.4
  48.6 19.7 %all_to_all.18.mine_ref = f32[16,144,128]{2,1,0:T(8,128)S(1)} all-to-all(f32[16,144,128]{2,1,0:T(8,128)S(1)} %shard_map.84), channel_id=1, replica_groups={{0,2,4,6,8,10,12,14,16,18,20,22,24,26,28,30},{1,3,5,7,9,11,13,15,17,19,..., dimensions={0} | all-to-all | bytes 2359296 | tf_op jit(solution)/shard_map/all_to_all | solution.py:281
  68.3 4.9 %collective-permute-start = (f32[16,144,128]{2,1,0:T(8,128)S(1)}, f32[16,144,128]{2,1,0:T(8,128)S(1)}, u32[]{:S(2)}, u32[]{:S(2)}) collective-permute-start(f32[16,144,128]{2,1,0:T(8,128)S(1)} %all_to_all.18.mine_ref), channel_id=1, source_target_pairs={{0,1},{1,0},{2,3},{3,2},{4,5},{5,4},{6,7},{7,6},{8,9},{9,8},{10,11... | collective-permute-start | bytes 3538952 | tf_op jit(solution)/shard_map/ppermute | solution.py:326
  73.2 2.5 %collective-permute-done.other_ref = f32[16,144,128]{2,1,0:T(8,128)S(1)} collective-permute-done((f32[16,144,128]{2,1,0:T(8,128)S(1)}, f32[16,144,128]{2,1,0:T(8,128)S(1)}, u32[]{:S(2)}, u32[]{:S(2)}) %collective-permute-start) | collective-permute-done | bytes 1179680 | tf_op jit(solution)/shard_map/ppermute | solution.py:326
  75.7 0.0 copy-done.3
  75.7 0.0 copy-done.4
  75.7 19.6 %shard_map.85 = f32[1,256]{1,0:T(1,128)} custom-call(f32[16,144,128]{2,1,0:T(8,128)S(1)} %all_to_all.18.mine_ref, f32[16,144,128]{2,1,0:T(8,128)S(1)} %collective-permute-done.other_ref, f32[1,256]{1,0:T(1,128)S(1)} %bitcast.2, f32[1,256]{1,0:T(1,128)S(1)} %bitcast.3), custom_call_target="tpu_custom_call" | custom-call | tf_op jit(solution)/shard_map/pallas_call | solution.py:260
Async XLA Ops:
  0.7 1.0 %copy-start = (bf16[1,1024,256]{2,1,0:T(8,128)(2,1)S(1)}, bf16[1,1024,256]{2,1,0:T(8,128)(2,1)}, u32[]{:S(2)}) copy-start(bf16[1,1024,256]{2,1,0:T(8,128)(2,1)} %basis_hbm.1) | copy-start | bytes 1572868
  1.7 0.7 copy-start.1
  2.4 0.7 copy-start.2
  3.1 0.7 copy-start.5
  3.7 0.7 copy-start.6
  48.5 27.2 %copy-start.3 = (f32[256]{0:T(256)S(1)}, f32[256]{0:T(256)}, u32[]{:S(2)}) copy-start(f32[256]{0:T(256)} %param.14) | copy-start | bytes 3076
  48.6 27.1 %copy-start.4 = (f32[256]{0:T(256)S(1)}, f32[256]{0:T(256)}, u32[]{:S(2)}) copy-start(f32[256]{0:T(256)} %param.15) | copy-start | bytes 3076
  68.3 7.4 %collective-permute-start = (f32[16,144,128]{2,1,0:T(8,128)S(1)}, f32[16,144,128]{2,1,0:T(8,128)S(1)}, u32[]{:S(2)}, u32[]{:S(2)}) collective-permute-start(f32[16,144,128]{2,1,0:T(8,128)S(1)} %all_to_all.18.mine_ref), channel_id=1, source_target_pairs={{0,1},{1,0},{2,3},{3,2},{4,5},{5,4},{6,7},{7,6},{8,9},{9,8},{10,11... | collective-permute-start | bytes 3538952 | tf_op jit(solution)/shard_map/ppermute | solution.py:326

commit v3 on v2

--- a/solution.py
+++ b/solution.py
@@ -227,27 +227,23 @@
     bound = size[0, 0] * (TOLERANCE * TOLERANCE)
 
     def unfinished(state):
-        return jnp.logical_and(state[0] < MOST_STEPS, state[6][0, 0] > bound)
+        return jnp.logical_and(state[0] < MOST_STEPS, state[4][0, 0] > bound)
 
     def step(state):
-        count, x, r, z, p, path, size, before, length = state
-        image = apply(z)
-        energy = inner(z, image)
-        ratio = jnp.where(before > 0.0, size / before, 0.0)
-        past = jnp.where(length > 0.0, ratio * size / length, 0.0)
-        energy = energy - past
+        count, x, r, p, size = state
+        image = apply(p)
+        energy = inner(p, image)
         length = jnp.where(energy > 0.0, size / energy, 0.0)
+        x = x + length * p
+        r = r - length * image
+        z = precondition(r)
+        fresh = inner(r, z)
+        ratio = jnp.where(size > 0.0, fresh / size, 0.0)
         p = z + ratio * p
-        path = image + ratio * path
-        x = x + length * p
-        r = r - length * path
-        z = precondition(r)
-        return (count + 1, x, r, z, p, path, inner(r, z), size, length)
+        return (count + 1, x, r, p, fresh)
 
     zero = jnp.zeros((epochs, width), jnp.float32)
-    none = jnp.zeros((1, 1), jnp.float32)
-    state = (0, zero, right, start, zero, zero, size, none, none)
-    solved = lax.while_loop(unfinished, step, state)[1]
+    solved = lax.while_loop(unfinished, step, (0, zero, right, start, size))[1]
     out_ref[...] = jnp.sum(jnp.where(index == epoch_here, solved, 0.0), axis=0, keepdims=True)
 
 
@@ -306,7 +302,7 @@
         (parts * SLAB, 1, HALF),
         [HBM] * 6,
         scratch,
-        16,
+        60,
         ray_count,
         station_var,
         ray_basis,

time: 95.7 us -> 90.5 us (0.946)
  local copies, waits for them, and re-layouts: 3.75 us -> 0.01 us
  Pallas kernels: 21.1 us -> 19.5 us
    unnamed x14 -> x4, local copies, waits for them, and re-layouts: 3.75 us -> 0.01 us
    pallas_call x4, Pallas kernels: 21.1 us -> 19.5 us  [call(): pl.pallas_call(kernel, out_shape=jax.ShapeDtypeStruct(shape, jnp.float32)...]
where the time goes in v3:
time: 90.5 us; the launch traced here: 90.2 us
  blocking collectives  62.6 us (69%)
  Pallas kernels  19.5 us (22%)
  starting transfers between devices  4.94 us (5%)
  waiting for transfers between devices  2.45 us (3%)
    all_to_all x3, blocking collectives, exchange(): lax.all_to_all(x, axis, split_axis=0, concat_axis=0, tiled=True, axis_ind...  62.6 us
    pallas_call x4, Pallas kernels, call(): pl.pallas_call(kernel, out_shape=jax.ShapeDtypeStruct(shape, jnp.float32)...  19.5 us
    ppermute x1, starting transfers between devices, shards(): lax.ppermute(mine, 'sta', [(i, i + 1 - 2 * (i % 2)) for i in range(parts)])  4.94 us
    ppermute x1, waiting for transfers between devices, shards(): lax.ppermute(mine, 'sta', [(i, i + 1 - 2 * (i % 2)) for i in range(parts)])  2.45 us
  transfers between devices with their start and end apart: 1, of which 1 were waited for; matrix products, arithmetic and copies ran while one was open for 0% of the time, Pallas kernels for 0%

profile of v3, /device:TPU:1, one launch (start us, length us, event | category | flops | bytes accessed | tf_op | source)
XLA Modules:
  0.0 90.2 jit_solution(4453583926788244136)
XLA Ops:
  0.7 2.4 %shard_map.82 = f32[288,1,128]{2,1,0:T(1,128)} custom-call(s32[1,1]{1,0:T(1,128)S(6)} %copy.9.count_hbm, f32[16]{0:T(128)} %var_hbm.1, bf16[1,1024,256]{2,1,0:T(8,128)(2,1)} %basis_hbm.1, bf16[1,1024]{1,0:T(2,128)(2,1)} %delay_hbm.1, s32[1,1024]{1,0:T(1,128)} %station_hbm.1, f32[1,256]{1,0:T(1,128)} %decay_hbm.1), custom_call_target="tpu_custom_call" | custom-call | tf_op jit(solution)/shard_map/pallas_call | solution.py:256
  3.1 18.3 %all_to_all.16.parts_ref = f32[288,1,128]{2,1,0:T(1,128)S(1)} all-to-all(f32[288,1,128]{2,1,0:T(1,128)} %shard_map.82), channel_id=1, replica_groups=mesh['tm'=16,'sta'=32] {'sta'}, dimensions={0} | all-to-all | bytes 294912 | tf_op jit(solution)/shard_map/all_to_all | solution.py:277
  21.4 0.1 shard_map.83
  21.5 24.5 %all_to_all.17.rows_ref = f32[144,1,128]{2,1,0:T(1,128)S(1)} all-to-all(f32[144,1,128]{2,1,0:T(1,128)S(1)} %shard_map.83), channel_id=1, replica_groups=mesh['tm'=16,'sta'=32] {'tm'}, dimensions={0} | all-to-all | bytes 147456 | tf_op jit(solution)/shard_map/all_to_all | solution.py:277
  46.0 0.1 shard_map.84
  46.2 0.0 copy-start
  46.2 0.0 copy-start.1
  46.2 19.7 %all_to_all.18.mine_ref = f32[16,144,128]{2,1,0:T(8,128)S(1)} all-to-all(f32[16,144,128]{2,1,0:T(8,128)S(1)} %shard_map.84), channel_id=1, replica_groups={{0,2,4,6,8,10,12,14,16,18,20,22,24,26,28,30},{1,3,5,7,9,11,13,15,17,19,..., dimensions={0} | all-to-all | bytes 2359296 | tf_op jit(solution)/shard_map/all_to_all | solution.py:277
  65.9 4.9 %collective-permute-start = (f32[16,144,128]{2,1,0:T(8,128)S(1)}, f32[16,144,128]{2,1,0:T(8,128)S(1)}, u32[]{:S(2)}, u32[]{:S(2)}) collective-permute-start(f32[16,144,128]{2,1,0:T(8,128)S(1)} %all_to_all.18.mine_ref), channel_id=1, source_target_pairs={{0,1},{1,0},{2,3},{3,2},{4,5},{5,4},{6,7},{7,6},{8,9},{9,8},{10,11... | collective-permute-start | bytes 3538952 | tf_op jit(solution)/shard_map/ppermute | solution.py:322
  70.9 2.5 %collective-permute-done.other_ref = f32[16,144,128]{2,1,0:T(8,128)S(1)} collective-permute-done((f32[16,144,128]{2,1,0:T(8,128)S(1)}, f32[16,144,128]{2,1,0:T(8,128)S(1)}, u32[]{:S(2)}, u32[]{:S(2)}) %collective-permute-start) | collective-permute-done | bytes 1179680 | tf_op jit(solution)/shard_map/ppermute | solution.py:322
  73.3 0.0 copy-done
  73.3 0.0 copy-done.1
  73.3 16.8 %shard_map.85 = f32[1,256]{1,0:T(1,128)} custom-call(f32[16,144,128]{2,1,0:T(8,128)S(1)} %all_to_all.18.mine_ref, f32[16,144,128]{2,1,0:T(8,128)S(1)} %collective-permute-done.other_ref, f32[1,256]{1,0:T(1,128)S(1)} %bitcast.2, f32[1,256]{1,0:T(1,128)S(1)} %bitcast.3), custom_call_target="tpu_custom_call" | custom-call | tf_op jit(solution)/shard_map/pallas_call | solution.py:256
Async XLA Ops:
  46.2 27.2 %copy-start = (f32[256]{0:T(256)S(1)}, f32[256]{0:T(256)}, u32[]{:S(2)}) copy-start(f32[256]{0:T(256)} %param.14) | copy-start | bytes 3076
  46.2 27.1 %copy-start.1 = (f32[256]{0:T(256)S(1)}, f32[256]{0:T(256)}, u32[]{:S(2)}) copy-start(f32[256]{0:T(256)} %param.15) | copy-start | bytes 3076
  65.9 7.4 %collective-permute-start = (f32[16,144,128]{2,1,0:T(8,128)S(1)}, f32[16,144,128]{2,1,0:T(8,128)S(1)}, u32[]{:S(2)}, u32[]{:S(2)}) collective-permute-start(f32[16,144,128]{2,1,0:T(8,128)S(1)} %all_to_all.18.mine_ref), channel_id=1, source_target_pairs={{0,1},{1,0},{2,3},{3,2},{4,5},{5,4},{6,7},{7,6},{8,9},{9,8},{10,11... | collective-permute-start | bytes 3538952 | tf_op jit(solution)/shard_map/ppermute | solution.py:322

commit v4 on v3

--- a/solution.py
+++ b/solution.py
@@ -73,11 +73,13 @@
     second = information[HALF:, HALF:]
     row = lax.broadcasted_iota(jnp.int32, (HALF, HALF), 0)
     col = lax.broadcasted_iota(jnp.int32, (HALF, HALF), 1)
-    diagonal = jnp.sum(jnp.where(row == col, second, 0.0), axis=0, keepdims=True)
+    diagonals = [
+        jnp.sum(jnp.where(row == col, block, 0.0), axis=0, keepdims=True) for block in (first, second)
+    ]
     triangles = jnp.where(col >= row, first, second)
     corner = information[:HALF, HALF:]
     own = jnp.where(shard == 0, decay_ref[...], 0.0)
-    extras = [drive[:, :HALF], drive[:, HALF:], diagonal, own[:, :HALF], own[:, HALF:]]
+    extras = [drive[:, :HALF], drive[:, HALF:], *diagonals, own[:, :HALF], own[:, HALF:]]
     blank = jnp.zeros((1, HALF), jnp.float32)
     for j in range(HALF // TILE):
         extra = extras[j] if j < len(extras) else blank
@@ -110,56 +112,45 @@
             out_ref[j, epochs * TILE + k : epochs * TILE + k + 1, :] = extra
 
 
-def solve_kernel(
-    mine_ref,
-    other_ref,
-    spread_ref,
-    prior_ref,
-    out_ref,
-    packed,
-    high,
-    low,
-    response,
-):
-    epochs, _, width = response.shape
-    chips = mine_ref.shape[0]
-    core = lax.rem(lax.axis_index("sta"), 2)
-    epoch_here = lax.axis_index("tm")
+def unpack(slabs_ref, triangles, high, low, epochs, width):
+    chips = slabs_ref.shape[0]
     row = lax.broadcasted_iota(jnp.int32, (HALF, HALF), 0)
     col = lax.broadcasted_iota(jnp.int32, (HALF, HALF), 1)
 
-    def unpack(e, carry):
+    def one(e, carry):
         place = pl.multiple_of(e * TILE, TILE)
-        for j in range(chips):
-            ours = pl.multiple_of(core * HALF + j * TILE, TILE)
-            theirs = pl.multiple_of((1 - core) * HALF + j * TILE, TILE)
-            packed[pl.ds(ours, TILE), :] = mine_ref[j, pl.ds(place, TILE), :]
-            packed[pl.ds(theirs, TILE), :] = other_ref[j, pl.ds(place, TILE), :]
-        triangles = packed[:HALF, :]
-        corner = packed[HALF:, :]
-        turned = triangles.T
-        on_diagonal = row == col
-        own = jnp.sum(jnp.where(on_diagonal, triangles, 0.0), axis=0, keepdims=True)
-        first = jnp.where(on_diagonal, 0.0, jnp.where(col > row, triangles, turned))
-        second = jnp.where(on_diagonal, 0.0, jnp.where(col < row, triangles, turned))
-        base = pl.multiple_of(e * width, width)
-        for r, c, block in ((0, 0, first), (0, 1, corner), (1, 0, corner.T), (1, 1, second)):
-            rows = pl.ds(base + r * HALF, HALF)
-            lanes = slice(c * HALF, c * HALF + HALF)
-            upper = block.astype(jnp.bfloat16)
-            high[rows, lanes] = upper
-            low[rows, lanes] = (block - upper.astype(jnp.float32)).astype(jnp.bfloat16)
-        return jnp.where(epoch_rows == e, own, carry)
-
-    epoch_rows = lax.broadcasted_iota(jnp.int32, (epochs, HALF), 0)
-    corner_diagonal = lax.fori_loop(0, epochs, unpack, jnp.zeros((epochs, HALF), jnp.float32))
+        block = jnp.concatenate(
+            [slabs_ref[j, pl.ds(place, TILE), :] for j in range(chips)], axis=0
+        )
+        turned = block.T
+        pair = (block, turned)
+        if triangles:
+            pair = (
+                jnp.where(row == col, 0.0, jnp.where(col > row, block, turned)),
+                jnp.where(row == col, 0.0, jnp.where(col < row, block, turned)),
+            )
+        for r in range(2):
+            rows = pl.ds(pl.multiple_of(e * width + r * HALF, HALF), HALF)
+            lane = (r if triangles else 1 - r) * HALF
+            upper = pair[r].astype(jnp.bfloat16)
+            high[rows, lane : lane + HALF] = upper
+            low[rows, lane : lane + HALF] = (pair[r] - upper.astype(jnp.float32)).astype(jnp.bfloat16)
+        return carry
+
+    lax.fori_loop(0, epochs, one, 0, unroll=4)
+
+
+def prepare_kernel(mine_ref, spread_ref, prior_ref, high, low, response, system):
+    epochs, _, width = response.shape
+    core = lax.rem(lax.axis_index("sta"), 2)
+    pl.when(core == 0)(lambda: unpack(mine_ref, True, high, low, epochs, width))
+    pl.when(core == 1)(lambda: unpack(mine_ref, False, high, low, epochs, width))
 
     def extra(k):
-        return mine_ref[k, epochs * TILE : epochs * TILE + epochs, :]
-
-    drive = jnp.concatenate([extra(0), extra(1)], axis=1)
-    decay = jnp.concatenate([extra(3), extra(4)], axis=1)
-    diagonal = jnp.concatenate([corner_diagonal, extra(2)], axis=1)
+        rows = slice(epochs * TILE, epochs * TILE + epochs)
+        return jnp.concatenate([mine_ref[k, rows, :], mine_ref[k + 1, rows, :]], axis=1)
+
+    drive, diagonal, decay = extra(0), extra(2), extra(4)
     inverse_noise = 1.0 / ((1.0 - decay * decay) * spread_ref[...])
     index = lax.broadcasted_iota(jnp.int32, (epochs, width), 0)
     pull = decay * inverse_noise
@@ -168,6 +159,10 @@
     carried = jnp.where(index == epochs - 1, 0.0, pltpu.roll(decay * pull, epochs - 1, 0))
     middle = inverse_noise + carried + diagonal
     right = drive + jnp.where(index == 0, pull * prior_ref[...], 0.0)
+    system[0] = middle
+    system[1] = link
+    system[2] = link_back
+    system[3] = right
 
     at = lambda x, e: x[e : e + 1, :]
     ahead = [at(middle, 0)]
@@ -196,6 +191,17 @@
         response[e] = response[e] + above
         above = jnp.where(index == e, centre[e], above)
 
+
+def solve_kernel(other_ref, high_in, low_in, response, system, out_ref, high, low):
+    epochs, _, width = response.shape
+    core = lax.rem(lax.axis_index("sta"), 2)
+    epoch_here = lax.axis_index("tm")
+    pl.when(core == 0)(lambda: unpack(other_ref, False, high, low, epochs, width))
+    pl.when(core == 1)(lambda: unpack(other_ref, True, high, low, epochs, width))
+    middle, link, link_back, right = (system[k] for k in range(4))
+    index = lax.broadcasted_iota(jnp.int32, (epochs, width), 0)
+    at = lambda x, e: x[e : e + 1, :]
+
     def precondition(r):
         total = at(r, 0) * response[0]
         for e in range(1, epochs):
@@ -255,7 +261,7 @@
 def call(kernel, shape, specs, scratch, vmem, *operands):
     return pl.pallas_call(
         kernel,
-        out_shape=jax.ShapeDtypeStruct(shape, jnp.float32),
+        out_shape=pltpu.VMEM(shape, jnp.float32),
         in_specs=specs,
         out_specs=VMEM,
         scratch_shapes=scratch,
@@ -264,13 +270,27 @@
 
 
 def solve(mine, other, spread, prior, epochs, width):
-    scratch = [
-        pltpu.VMEM((width, HALF), jnp.float32),
-        pltpu.VMEM((epochs * width, width), jnp.bfloat16),
-        pltpu.VMEM((epochs * width, width), jnp.bfloat16),
+    halves = [pltpu.VMEM((epochs * width, width), jnp.bfloat16)] * 2
+    tables = [
         pltpu.VMEM((epochs, epochs, width), jnp.float32),
+        pltpu.VMEM((4, epochs, width), jnp.float32),
     ]
-    return call(solve_kernel, (1, width), [VMEM] * 4, scratch, 24, mine, other, spread, prior)
+    high, low, response, system = pl.pallas_call(
+        prepare_kernel,
+        out_shape=halves + tables,
+        in_specs=[VMEM] * 3,
+        out_specs=[VMEM] * 4,
+        compiler_params=pltpu.CompilerParams(vmem_limit_bytes=8 * MIB),
+        cost_estimate=pl.CostEstimate(flops=2**24, bytes_accessed=2**22, transcendentals=0),
+    )(mine, spread, prior)
+    return pl.pallas_call(
+        solve_kernel,
+        out_shape=[jax.ShapeDtypeStruct((1, width), jnp.float32)] + halves,
+        in_specs=[VMEM] * 5,
+        out_specs=[VMEM] * 3,
+        input_output_aliases={1: 1, 2: 2},
+        compiler_params=pltpu.CompilerParams(vmem_limit_bytes=8 * MIB),
+    )(other, high, low, response, system)[0]
 
 
 def exchange(x, axis, groups=None):

time: 90.5 us -> 88.8 us (0.981)
  waiting for transfers between devices: 2.45 us -> 1.51 us
    ppermute x1, waiting for transfers between devices: 2.45 us -> 1.51 us  [shards(): lax.ppermute(mine, 'sta', [(i, i + 1 - 2 * (i % 2)) for i in range(parts)])]
    pallas_call x4 -> x5, Pallas kernels: 19.5 us -> 19 us  [the longest x1 16.1 us: solve(): pl.pallas_call(solve_kernel, out_shape=[jax.ShapeDtypeStruct((1, width),...]
  transfers between devices with their start and end apart: 1 -> 1, of which waited for: 1 -> 1; matrix products, arithmetic and copies ran while one was open for 0% -> 0% of each run, Pallas kernels for 0% -> 1%
where the time goes in v4:
time: 88.8 us; the launch traced here: 88.6 us
  blocking collectives  62.4 us (70%)
  Pallas kernels  19 us (21%)
  starting transfers between devices  4.94 us (6%)
  waiting for transfers between devices  1.51 us (2%)
    all_to_all x3, blocking collectives, exchange(): lax.all_to_all(x, axis, split_axis=0, concat_axis=0, tiled=True, axis_ind...  62.4 us
    pallas_call x1, Pallas kernels, solve(): pl.pallas_call(solve_kernel, out_shape=[jax.ShapeDtypeStruct((1, width),...  16.1 us
    ppermute x1, starting transfers between devices, shards(): lax.ppermute(mine, 'sta', [(i, i + 1 - 2 * (i % 2)) for i in range(parts)])  4.94 us
    pallas_call x3, Pallas kernels, call(): pl.pallas_call(kernel, out_shape=pltpu.VMEM(shape, jnp.float32), in_specs...  2.01 us
  transfers between devices with their start and end apart: 1, of which 1 were waited for; matrix products, arithmetic and copies ran while one was open for 0% of the time, Pallas kernels for 1%

profile of v4, /device:TPU:1, one launch (start us, length us, event | category | flops | bytes accessed | tf_op | source)
XLA Modules:
  0.0 88.6 jit_solution(12929575163566880424)
XLA Ops:
  0.7 1.8 %shard_map.82 = f32[288,1,128]{2,1,0:T(1,128)S(1)} custom-call(s32[1,1]{1,0:T(1,128)S(6)} %copy.13.count_hbm, f32[16]{0:T(128)} %var_hbm.1, bf16[1,1024,256]{2,1,0:T(8,128)(2,1)} %basis_hbm.1, bf16[1,1024]{1,0:T(2,128)(2,1)} %delay_hbm.1, s32[1,1024]{1,0:T(1,128)} %station_hbm.1, f32[1,256]{1,0:T(1,128)} %decay_hbm.1), custom_call_target="tpu_custom_call" | custom-call | tf_op jit(solution)/shard_map/pallas_call | solution.py:262
  2.4 0.0 copy-start
  2.5 0.0 copy-start.1
  2.5 17.4 %all_to_all.16.parts_ref = f32[288,1,128]{2,1,0:T(1,128)S(1)} all-to-all(f32[288,1,128]{2,1,0:T(1,128)S(1)} %shard_map.82), channel_id=1, replica_groups=mesh['tm'=16,'sta'=32] {'sta'}, dimensions={0} | all-to-all | bytes 294912 | tf_op jit(solution)/shard_map/all_to_all | solution.py:297
  19.9 0.1 shard_map.83
  20.0 25.2 %all_to_all.17.rows_ref = f32[144,1,128]{2,1,0:T(1,128)S(1)} all-to-all(f32[144,1,128]{2,1,0:T(1,128)S(1)} %shard_map.83), channel_id=1, replica_groups=mesh['tm'=16,'sta'=32] {'tm'}, dimensions={0} | all-to-all | bytes 147456 | tf_op jit(solution)/shard_map/all_to_all | solution.py:297
  45.2 0.1 shard_map.84
  45.3 19.7 %all_to_all.18.mine_ref = f32[16,144,128]{2,1,0:T(8,128)S(1)} all-to-all(f32[16,144,128]{2,1,0:T(8,128)S(1)} %shard_map.84), channel_id=1, replica_groups={{0,2,4,6,8,10,12,14,16,18,20,22,24,26,28,30},{1,3,5,7,9,11,13,15,17,19,..., dimensions={0} | all-to-all | bytes 2359296 | tf_op jit(solution)/shard_map/all_to_all | solution.py:297
  65.1 4.9 %collective-permute-start = (f32[16,144,128]{2,1,0:T(8,128)S(1)}, f32[16,144,128]{2,1,0:T(8,128)S(1)}, u32[]{:S(2)}, u32[]{:S(2)}) collective-permute-start(f32[16,144,128]{2,1,0:T(8,128)S(1)} %all_to_all.18.mine_ref), channel_id=1, source_target_pairs={{0,1},{1,0},{2,3},{3,2},{4,5},{5,4},{6,7},{7,6},{8,9},{9,8},{10,11... | collective-permute-start | bytes 3538952 | tf_op jit(solution)/shard_map/ppermute | solution.py:342
  70.0 0.0 copy-done
  70.0 0.0 copy-done.1
  70.0 0.9 %shard_map.85 = (bf16[4096,256]{1,0:T(8,128)(2,1)S(1)}, bf16[4096,256]{1,0:T(8,128)(2,1)S(1)}, f32[16,16,256]{2,1,0:T(8,128)S(1)}, f32[4,16,256]{2,1,0:T(8,128)S(1)}) custom-call(f32[16,144,128]{2,1,0:T(8,128)S(1)} %all_to_all.18.mine_ref, f32[1,256]{1,0:T(1,128)S(1)} %bitcast.2, f32[1,256]{1,0:T(1,128)S(1)} %bitcast.3), custom_call_target="tpu_custom_call" | custom-call | flops 16777216 | bytes 4194304 | tf_op jit(solution)/shard_map/pallas_call | solution.py:278
  71.0 1.5 %collective-permute-done.other_ref = f32[16,144,128]{2,1,0:T(8,128)S(1)} collective-permute-done((f32[16,144,128]{2,1,0:T(8,128)S(1)}, f32[16,144,128]{2,1,0:T(8,128)S(1)}, u32[]{:S(2)}, u32[]{:S(2)}) %collective-permute-start) | collective-permute-done | bytes 1179680 | tf_op jit(solution)/shard_map/ppermute | solution.py:342
  72.5 16.1 %shard_map.86 = (f32[1,256]{1,0:T(1,128)}, bf16[4096,256]{1,0:T(8,128)(2,1)S(1)}, bf16[4096,256]{1,0:T(8,128)(2,1)S(1)}) custom-call(f32[16,144,128]{2,1,0:T(8,128)S(1)} %collective-permute-done.other_ref, bf16[4096,256]{1,0:T(8,128)(2,1)S(1)} %get-tuple-element.10.high_in, ...), custom_call_target="tpu_custom_call", output_to_operand_aliasing={{1}: (1, {}), {2}: (2, {})} | custom-call | tf_op jit(solution)/shard_map/pallas_call | solution.py:286
Async XLA Ops:
  2.4 67.6 %copy-start = (f32[256]{0:T(256)S(1)}, f32[256]{0:T(256)}, u32[]{:S(2)}) copy-start(f32[256]{0:T(256)} %param.14) | copy-start | bytes 3076
  2.5 67.6 %copy-start.1 = (f32[256]{0:T(256)S(1)}, f32[256]{0:T(256)}, u32[]{:S(2)}) copy-start(f32[256]{0:T(256)} %param.15) | copy-start | bytes 3076
  65.1 7.4 %collective-permute-start = (f32[16,144,128]{2,1,0:T(8,128)S(1)}, f32[16,144,128]{2,1,0:T(8,128)S(1)}, u32[]{:S(2)}, u32[]{:S(2)}) collective-permute-start(f32[16,144,128]{2,1,0:T(8,128)S(1)} %all_to_all.18.mine_ref), channel_id=1, source_target_pairs={{0,1},{1,0},{2,3},{3,2},{4,5},{5,4},{6,7},{7,6},{8,9},{9,8},{10,11... | collective-permute-start | bytes 3538952 | tf_op jit(solution)/shard_map/ppermute | solution.py:342

commit v5 on v4

--- a/solution.py
+++ b/solution.py
@@ -8,7 +8,8 @@
 HALF = 128
 TILE = 8
 SLAB = TILE + 1
-TOLERANCE = 1e-5
+TOLERANCE = 2e-5
+PIECES = 4
 MOST_STEPS = 4000
 
 
@@ -43,10 +44,16 @@
             )
         )
     ]
-    whole = pltpu.make_async_copy(basis_hbm.at[0], basis_ref, arrived.at[len(small)])
-    for copy in small:
+    large = [
+        pltpu.make_async_copy(
+            basis_hbm.at[0, pl.ds(k * rays // PIECES, rays // PIECES)],
+            basis_ref.at[pl.ds(k * rays // PIECES, rays // PIECES)],
+            arrived.at[len(small) + k],
+        )
+        for k in range(PIECES)
+    ]
+    for copy in small + large:
         copy.start()
-    whole.start()
     shard = lax.axis_index("sta")
     for copy in small:
         copy.wait()
@@ -56,8 +63,9 @@
         variance = jnp.where(local == k, var_ref[k], variance)
     slot = lax.broadcasted_iota(jnp.int32, local.shape, 1)
     weight = jnp.where(slot < count_ref[0, 0], 1.0 / variance, 0.0)
-    whole.wait()
     for start in range(0, rays, HALF):
+        if start % (rays // PIECES) == 0:
+            large[start * PIECES // rays].wait()
         rows = slice(start, start + HALF)
         column = jnp.broadcast_to(weight[:, rows], (HALF, HALF)).T
         for lane in (0, HALF):
@@ -233,10 +241,11 @@
     bound = size[0, 0] * (TOLERANCE * TOLERANCE)
 
     def unfinished(state):
-        return jnp.logical_and(state[0] < MOST_STEPS, state[4][0, 0] > bound)
+        return jnp.logical_and(state[0] < MOST_STEPS, state[1])
 
     def step(state):
-        count, x, r, p, size = state
+        count, _, x, r, p, size = state
+        again = size[0, 0] > bound
         image = apply(p)
         energy = inner(p, image)
         length = jnp.where(energy > 0.0, size / energy, 0.0)
@@ -246,10 +255,10 @@
         fresh = inner(r, z)
         ratio = jnp.where(size > 0.0, fresh / size, 0.0)
         p = z + ratio * p
-        return (count + 1, x, r, p, fresh)
+        return (count + 1, again, x, r, p, fresh)
 
     zero = jnp.zeros((epochs, width), jnp.float32)
-    solved = lax.while_loop(unfinished, step, (0, zero, right, start, size))[1]
+    solved = lax.while_loop(unfinished, step, (0, True, zero, right, start, size))[2]
     out_ref[...] = jnp.sum(jnp.where(index == epoch_here, solved, 0.0), axis=0, keepdims=True)
 
 
@@ -315,7 +324,7 @@
         pltpu.VMEM((1, rays), jnp.int32),
         pltpu.VMEM((1, width), jnp.float32),
         pltpu.VMEM((rays, width), jnp.bfloat16),
-        pltpu.SemaphoreType.DMA((6,)),
+        pltpu.SemaphoreType.DMA((5 + PIECES,)),
     ]
     share = call(
         ray_kernel,

time: 88.8 us -> 87.5 us (0.985)
  Pallas kernels: 19 us -> 17.7 us
    pallas_call x1, Pallas kernels: 16.1 us -> 14.8 us  [solve(): pl.pallas_call(solve_kernel, out_shape=[jax.ShapeDtypeStruct((1, width),...]
where the time goes in v5:
time: 87.5 us; the launch traced here: 87.3 us
  blocking collectives  62.4 us (71%)
  Pallas kernels  17.7 us (20%)
  starting transfers between devices  4.94 us (6%)
  waiting for transfers between devices  1.51 us (2%)
    all_to_all x3, blocking collectives, exchange(): lax.all_to_all(x, axis, split_axis=0, concat_axis=0, tiled=True, axis_ind...  62.4 us
    pallas_call x1, Pallas kernels, solve(): pl.pallas_call(solve_kernel, out_shape=[jax.ShapeDtypeStruct((1, width),...  14.8 us
    ppermute x1, starting transfers between devices, shards(): lax.ppermute(mine, 'sta', [(i, i + 1 - 2 * (i % 2)) for i in range(parts)])  4.94 us
    pallas_call x3, Pallas kernels, call(): pl.pallas_call(kernel, out_shape=pltpu.VMEM(shape, jnp.float32), in_specs...  2.05 us
  transfers between devices with their start and end apart: 1, of which 1 were waited for; matrix products, arithmetic and copies ran while one was open for 0% of the time, Pallas kernels for 1%

profile of v5, /device:TPU:1, one launch (start us, length us, event | category | flops | bytes accessed | tf_op | source)
XLA Modules:
  0.0 87.3 jit_solution(1125860381243274523)
XLA Ops:
  0.7 1.8 %shard_map.82 = f32[288,1,128]{2,1,0:T(1,128)S(1)} custom-call(s32[1,1]{1,0:T(1,128)S(6)} %copy.13.count_hbm, f32[16]{0:T(128)} %var_hbm.1, bf16[1,1024,256]{2,1,0:T(8,128)(2,1)} %basis_hbm.1, bf16[1,1024]{1,0:T(2,128)(2,1)} %delay_hbm.1, s32[1,1024]{1,0:T(1,128)} %station_hbm.1, f32[1,256]{1,0:T(1,128)} %decay_hbm.1), custom_call_target="tpu_custom_call" | custom-call | tf_op jit(solution)/shard_map/pallas_call | solution.py:271
  2.5 0.0 copy-start
  2.5 0.0 copy-start.1
  2.5 17.4 %all_to_all.16.parts_ref = f32[288,1,128]{2,1,0:T(1,128)S(1)} all-to-all(f32[288,1,128]{2,1,0:T(1,128)S(1)} %shard_map.82), channel_id=1, replica_groups=mesh['tm'=16,'sta'=32] {'sta'}, dimensions={0} | all-to-all | bytes 294912 | tf_op jit(solution)/shard_map/all_to_all | solution.py:306
  19.9 0.1 shard_map.83
  20.0 25.2 %all_to_all.17.rows_ref = f32[144,1,128]{2,1,0:T(1,128)S(1)} all-to-all(f32[144,1,128]{2,1,0:T(1,128)S(1)} %shard_map.83), channel_id=1, replica_groups=mesh['tm'=16,'sta'=32] {'tm'}, dimensions={0} | all-to-all | bytes 147456 | tf_op jit(solution)/shard_map/all_to_all | solution.py:306
  45.2 0.1 shard_map.84
  45.4 19.7 %all_to_all.18.mine_ref = f32[16,144,128]{2,1,0:T(8,128)S(1)} all-to-all(f32[16,144,128]{2,1,0:T(8,128)S(1)} %shard_map.84), channel_id=1, replica_groups={{0,2,4,6,8,10,12,14,16,18,20,22,24,26,28,30},{1,3,5,7,9,11,13,15,17,19,..., dimensions={0} | all-to-all | bytes 2359296 | tf_op jit(solution)/shard_map/all_to_all | solution.py:306
  65.1 4.9 %collective-permute-start = (f32[16,144,128]{2,1,0:T(8,128)S(1)}, f32[16,144,128]{2,1,0:T(8,128)S(1)}, u32[]{:S(2)}, u32[]{:S(2)}) collective-permute-start(f32[16,144,128]{2,1,0:T(8,128)S(1)} %all_to_all.18.mine_ref), channel_id=1, source_target_pairs={{0,1},{1,0},{2,3},{3,2},{4,5},{5,4},{6,7},{7,6},{8,9},{9,8},{10,11... | collective-permute-start | bytes 3538952 | tf_op jit(solution)/shard_map/ppermute | solution.py:351
  70.0 0.0 copy-done
  70.1 0.0 copy-done.1
  70.1 0.9 %shard_map.85 = (bf16[4096,256]{1,0:T(8,128)(2,1)S(1)}, bf16[4096,256]{1,0:T(8,128)(2,1)S(1)}, f32[16,16,256]{2,1,0:T(8,128)S(1)}, f32[4,16,256]{2,1,0:T(8,128)S(1)}) custom-call(f32[16,144,128]{2,1,0:T(8,128)S(1)} %all_to_all.18.mine_ref, f32[1,256]{1,0:T(1,128)S(1)} %bitcast.2, f32[1,256]{1,0:T(1,128)S(1)} %bitcast.3), custom_call_target="tpu_custom_call" | custom-call | flops 16777216 | bytes 4194304 | tf_op jit(solution)/shard_map/pallas_call | solution.py:287
  71.0 1.5 %collective-permute-done.other_ref = f32[16,144,128]{2,1,0:T(8,128)S(1)} collective-permute-done((f32[16,144,128]{2,1,0:T(8,128)S(1)}, f32[16,144,128]{2,1,0:T(8,128)S(1)}, u32[]{:S(2)}, u32[]{:S(2)}) %collective-permute-start) | collective-permute-done | bytes 1179680 | tf_op jit(solution)/shard_map/ppermute | solution.py:351
  72.5 14.8 %shard_map.86 = (f32[1,256]{1,0:T(1,128)}, bf16[4096,256]{1,0:T(8,128)(2,1)S(1)}, bf16[4096,256]{1,0:T(8,128)(2,1)S(1)}) custom-call(f32[16,144,128]{2,1,0:T(8,128)S(1)} %collective-permute-done.other_ref, bf16[4096,256]{1,0:T(8,128)(2,1)S(1)} %get-tuple-element.10.high_in, ...), custom_call_target="tpu_custom_call", output_to_operand_aliasing={{1}: (1, {}), {2}: (2, {})} | custom-call | tf_op jit(solution)/shard_map/pallas_call | solution.py:295
Async XLA Ops:
  2.5 67.6 %copy-start = (f32[256]{0:T(256)S(1)}, f32[256]{0:T(256)}, u32[]{:S(2)}) copy-start(f32[256]{0:T(256)} %param.14) | copy-start | bytes 3076
  2.5 67.6 %copy-start.1 = (f32[256]{0:T(256)S(1)}, f32[256]{0:T(256)}, u32[]{:S(2)}) copy-start(f32[256]{0:T(256)} %param.15) | copy-start | bytes 3076
  65.1 7.4 %collective-permute-start = (f32[16,144,128]{2,1,0:T(8,128)S(1)}, f32[16,144,128]{2,1,0:T(8,128)S(1)}, u32[]{:S(2)}, u32[]{:S(2)}) collective-permute-start(f32[16,144,128]{2,1,0:T(8,128)S(1)} %all_to_all.18.mine_ref), channel_id=1, source_target_pairs={{0,1},{1,0},{2,3},{3,2},{4,5},{5,4},{6,7},{7,6},{8,9},{9,8},{10,11... | collective-permute-start | bytes 3538952 | tf_op jit(solution)/shard_map/ppermute | solution.py:351

commit v6 on v5

--- a/solution.py
+++ b/solution.py
@@ -9,6 +9,8 @@
 TILE = 8
 SLAB = TILE + 1
 TOLERANCE = 2e-5
+COARSE = 5e-2
+SHORT_STEPS = 24
 PIECES = 4
 MOST_STEPS = 4000
 
@@ -216,49 +218,79 @@
             total = total + at(r, e) * response[e]
         return total
 
-    def apply(p):
-        blocks = []
-        for e in range(epochs):
-            kept = jnp.where(index == e, p, 0.0)
-            upper = kept.astype(jnp.bfloat16)
-            rest = (kept - upper.astype(jnp.float32)).astype(jnp.bfloat16)
-            blocks.append(jnp.concatenate([upper, rest], axis=0))
-        left = jnp.concatenate(blocks, axis=1)
-        by_high = jnp.dot(left, high[...], preferred_element_type=jnp.float32)
-        by_low = jnp.dot(left[:epochs], low[...], preferred_element_type=jnp.float32)
+    def spread_rows(p):
+        upper = p.astype(jnp.bfloat16).astype(jnp.float32)
+        rest = p - upper
+        which = lax.rem(lax.broadcasted_iota(jnp.int32, (2 * TILE, width), 0), TILE)
+        lefts = []
+        for g in range(0, epochs, TILE):
+            both = jnp.concatenate([upper[g : g + TILE], rest[g : g + TILE]], axis=0)
+            pieces = [jnp.where(which == e, both, 0.0).astype(jnp.bfloat16) for e in range(TILE)]
+            lefts.append(jnp.concatenate(pieces, axis=1))
+        return lefts
+
+    def products(lefts, halves):
+        groups = []
+        for k, left in enumerate(lefts):
+            rows = slice(k * TILE * width, (k + 1) * TILE * width)
+            by = sum(jnp.dot(left, h[rows], preferred_element_type=jnp.float32) for h in halves)
+            groups.append(by[:TILE] + by[TILE:])
+        return jnp.concatenate(groups, axis=0)
+
+    def apply(p, halves):
         near = (
             middle * p
             - link * pltpu.roll(p, epochs - 1, 0)
             - link_back * pltpu.roll(p, 1, 0)
         )
-        return near + (by_high[:epochs] + by_high[epochs:] + by_low)
+        return near + products(spread_rows(p), halves)
 
     def inner(a, b):
         return jnp.sum(jnp.sum(a * b, axis=0, keepdims=True), axis=1, keepdims=True)
+
+    def iterate(halves, most, bound, x, r, p, size):
+        def unfinished(state):
+            return jnp.logical_and(state[0] < most, state[1] > 0)
+
+        def step(state):
+            count, _, x, r, p, size = state
+            again = jnp.where(size[0, 0] > bound, 1, 0)
+            image = apply(p, halves)
+            energy = inner(p, image)
+            length = jnp.where(energy > 0.0, size / energy, 0.0)
+            x = x + length * p
+            r = r - length * image
+            z = precondition(r)
+            fresh = inner(r, z)
+            ratio = jnp.where(size > 0.0, fresh / size, 0.0)
+            p = z + ratio * p
+            return (count + 1, again, x, r, p, fresh)
+
+        return lax.while_loop(unfinished, step, (0, 1, x, r, p, size))[2:]
 
     start = precondition(right)
     size = inner(right, start)
     bound = size[0, 0] * (TOLERANCE * TOLERANCE)
-
-    def unfinished(state):
-        return jnp.logical_and(state[0] < MOST_STEPS, state[1])
-
-    def step(state):
-        count, _, x, r, p, size = state
-        again = size[0, 0] > bound
-        image = apply(p)
-        energy = inner(p, image)
-        length = jnp.where(energy > 0.0, size / energy, 0.0)
-        x = x + length * p
-        r = r - length * image
-        z = precondition(r)
-        fresh = inner(r, z)
-        ratio = jnp.where(size > 0.0, fresh / size, 0.0)
-        p = z + ratio * p
-        return (count + 1, again, x, r, p, fresh)
-
     zero = jnp.zeros((epochs, width), jnp.float32)
-    solved = lax.while_loop(unfinished, step, (0, True, zero, right, start, size))[2]
+    coarse = size[0, 0] * (COARSE * COARSE)
+    x, r, p, size = iterate((high, low), MOST_STEPS, coarse, zero, right, start, size)
+    change, left_over, _, _ = iterate((high,), SHORT_STEPS, bound, zero, r, p, size)
+    left_over = left_over - products(spread_rows(change), (low,))
+    reached = inner(left_over, precondition(left_over))
+    unsure = jnp.where(reached[0, 0] <= bound, 0, 1)
+
+    def refine(state):
+        _, solved = state
+        better = reached < size
+        r_now = jnp.where(better, left_over, r)
+        z_now = precondition(r_now)
+        solved = iterate(
+            (high, low), MOST_STEPS, bound, solved, r_now, z_now, inner(r_now, z_now)
+        )[0]
+        return (0, solved)
+
+    solved = jnp.where(reached < size, x + change, x)
+    solved = lax.while_loop(lambda state: state[0] > 0, refine, (unsure, solved))[1]
     out_ref[...] = jnp.sum(jnp.where(index == epoch_here, solved, 0.0), axis=0, keepdims=True)
 
 

time: 87.5 us -> 86.5 us (0.989)
  Pallas kernels: 17.7 us -> 16.7 us
    pallas_call x1, Pallas kernels: 14.8 us -> 13.7 us  [solve(): pl.pallas_call(solve_kernel, out_shape=[jax.ShapeDtypeStruct((1, width),...]
where the time goes in v6:
time: 86.5 us; the launch traced here: 86.2 us
  blocking collectives  62.4 us (72%)
  Pallas kernels  16.7 us (19%)
  starting transfers between devices  4.94 us (6%)
  waiting for transfers between devices  1.51 us (2%)
    all_to_all x3, blocking collectives, exchange(): lax.all_to_all(x, axis, split_axis=0, concat_axis=0, tiled=True, axis_ind...  62.4 us
    pallas_call x1, Pallas kernels, solve(): pl.pallas_call(solve_kernel, out_shape=[jax.ShapeDtypeStruct((1, width),...  13.7 us
    ppermute x1, starting transfers between devices, shards(): lax.ppermute(mine, 'sta', [(i, i + 1 - 2 * (i % 2)) for i in range(parts)])  4.94 us
    pallas_call x3, Pallas kernels, call(): pl.pallas_call(kernel, out_shape=pltpu.VMEM(shape, jnp.float32), in_specs...  2.05 us
  transfers between devices with their start and end apart: 1, of which 1 were waited for; matrix products, arithmetic and copies ran while one was open for 0% of the time, Pallas kernels for 1%

profile of v6, /device:TPU:1, one launch (start us, length us, event | category | flops | bytes accessed | tf_op | source)
XLA Modules:
  0.0 86.2 jit_solution(12573173276184553154)
XLA Ops:
  0.7 1.8 %shard_map.82 = f32[288,1,128]{2,1,0:T(1,128)S(1)} custom-call(s32[1,1]{1,0:T(1,128)S(6)} %copy.13.count_hbm, f32[16]{0:T(128)} %var_hbm.1, bf16[1,1024,256]{2,1,0:T(8,128)(2,1)} %basis_hbm.1, bf16[1,1024]{1,0:T(2,128)(2,1)} %delay_hbm.1, s32[1,1024]{1,0:T(1,128)} %station_hbm.1, f32[1,256]{1,0:T(1,128)} %decay_hbm.1), custom_call_target="tpu_custom_call" | custom-call | tf_op jit(solution)/shard_map/pallas_call | solution.py:303
  2.5 0.0 copy-start
  2.5 0.0 copy-start.1
  2.5 17.4 %all_to_all.16.parts_ref = f32[288,1,128]{2,1,0:T(1,128)S(1)} all-to-all(f32[288,1,128]{2,1,0:T(1,128)S(1)} %shard_map.82), channel_id=1, replica_groups=mesh['tm'=16,'sta'=32] {'sta'}, dimensions={0} | all-to-all | bytes 294912 | tf_op jit(solution)/shard_map/all_to_all | solution.py:338
  19.9 0.1 shard_map.83
  20.0 25.2 %all_to_all.17.rows_ref = f32[144,1,128]{2,1,0:T(1,128)S(1)} all-to-all(f32[144,1,128]{2,1,0:T(1,128)S(1)} %shard_map.83), channel_id=1, replica_groups=mesh['tm'=16,'sta'=32] {'tm'}, dimensions={0} | all-to-all | bytes 147456 | tf_op jit(solution)/shard_map/all_to_all | solution.py:338
  45.2 0.1 shard_map.84
  45.4 19.7 %all_to_all.18.mine_ref = f32[16,144,128]{2,1,0:T(8,128)S(1)} all-to-all(f32[16,144,128]{2,1,0:T(8,128)S(1)} %shard_map.84), channel_id=1, replica_groups={{0,2,4,6,8,10,12,14,16,18,20,22,24,26,28,30},{1,3,5,7,9,11,13,15,17,19,..., dimensions={0} | all-to-all | bytes 2359296 | tf_op jit(solution)/shard_map/all_to_all | solution.py:338
  65.1 4.9 %collective-permute-start = (f32[16,144,128]{2,1,0:T(8,128)S(1)}, f32[16,144,128]{2,1,0:T(8,128)S(1)}, u32[]{:S(2)}, u32[]{:S(2)}) collective-permute-start(f32[16,144,128]{2,1,0:T(8,128)S(1)} %all_to_all.18.mine_ref), channel_id=1, source_target_pairs={{0,1},{1,0},{2,3},{3,2},{4,5},{5,4},{6,7},{7,6},{8,9},{9,8},{10,11... | collective-permute-start | bytes 3538952 | tf_op jit(solution)/shard_map/ppermute | solution.py:383
  70.0 0.0 copy-done
  70.1 0.0 copy-done.1
  70.1 0.9 %shard_map.85 = (bf16[4096,256]{1,0:T(8,128)(2,1)S(1)}, bf16[4096,256]{1,0:T(8,128)(2,1)S(1)}, f32[16,16,256]{2,1,0:T(8,128)S(1)}, f32[4,16,256]{2,1,0:T(8,128)S(1)}) custom-call(f32[16,144,128]{2,1,0:T(8,128)S(1)} %all_to_all.18.mine_ref, f32[1,256]{1,0:T(1,128)S(1)} %bitcast.2, f32[1,256]{1,0:T(1,128)S(1)} %bitcast.3), custom_call_target="tpu_custom_call" | custom-call | flops 16777216 | bytes 4194304 | tf_op jit(solution)/shard_map/pallas_call | solution.py:319
  71.0 1.5 %collective-permute-done.other_ref = f32[16,144,128]{2,1,0:T(8,128)S(1)} collective-permute-done((f32[16,144,128]{2,1,0:T(8,128)S(1)}, f32[16,144,128]{2,1,0:T(8,128)S(1)}, u32[]{:S(2)}, u32[]{:S(2)}) %collective-permute-start) | collective-permute-done | bytes 1179680 | tf_op jit(solution)/shard_map/ppermute | solution.py:383
  72.5 13.7 %shard_map.86 = (f32[1,256]{1,0:T(1,128)}, bf16[4096,256]{1,0:T(8,128)(2,1)S(1)}, bf16[4096,256]{1,0:T(8,128)(2,1)S(1)}) custom-call(f32[16,144,128]{2,1,0:T(8,128)S(1)} %collective-permute-done.other_ref, bf16[4096,256]{1,0:T(8,128)(2,1)S(1)} %get-tuple-element.10.high_in, ...), custom_call_target="tpu_custom_call", output_to_operand_aliasing={{1}: (1, {}), {2}: (2, {})} | custom-call | tf_op jit(solution)/shard_map/pallas_call | solution.py:327
Async XLA Ops:
  2.5 67.6 %copy-start = (f32[256]{0:T(256)S(1)}, f32[256]{0:T(256)}, u32[]{:S(2)}) copy-start(f32[256]{0:T(256)} %param.14) | copy-start | bytes 3076
  2.5 67.6 %copy-start.1 = (f32[256]{0:T(256)S(1)}, f32[256]{0:T(256)}, u32[]{:S(2)}) copy-start(f32[256]{0:T(256)} %param.15) | copy-start | bytes 3076
  65.1 7.4 %collective-permute-start = (f32[16,144,128]{2,1,0:T(8,128)S(1)}, f32[16,144,128]{2,1,0:T(8,128)S(1)}, u32[]{:S(2)}, u32[]{:S(2)}) collective-permute-start(f32[16,144,128]{2,1,0:T(8,128)S(1)} %all_to_all.18.mine_ref), channel_id=1, source_target_pairs={{0,1},{1,0},{2,3},{3,2},{4,5},{5,4},{6,7},{7,6},{8,9},{9,8},{10,11... | collective-permute-start | bytes 3538952 | tf_op jit(solution)/shard_map/ppermute | solution.py:383

commit v7 on v6

--- a/solution.py
+++ b/solution.py
@@ -147,7 +147,7 @@
             low[rows, lane : lane + HALF] = (pair[r] - upper.astype(jnp.float32)).astype(jnp.bfloat16)
         return carry
 
-    lax.fori_loop(0, epochs, one, 0, unroll=4)
+    lax.fori_loop(0, epochs, one, 0, unroll=16)
 
 
 def prepare_kernel(mine_ref, spread_ref, prior_ref, high, low, response, system):
@@ -248,44 +248,58 @@
     def inner(a, b):
         return jnp.sum(jnp.sum(a * b, axis=0, keepdims=True), axis=1, keepdims=True)
 
-    def iterate(halves, most, bound, x, r, p, size):
+    zero = jnp.zeros((epochs, width), jnp.float32)
+    none = jnp.zeros((1, 1), jnp.float32)
+
+    def iterate(halves, most, bound, x, r, z, p, path, before, length):
         def unfinished(state):
             return jnp.logical_and(state[0] < most, state[1] > 0)
 
         def step(state):
-            count, _, x, r, p, size = state
+            count, _, x, r, z, p, path, before, length = state
+            size = inner(r, z)
             again = jnp.where(size[0, 0] > bound, 1, 0)
-            image = apply(p, halves)
-            energy = inner(p, image)
+            image = apply(z, halves)
+            ratio = jnp.where(before > 0.0, size / before, 0.0)
+            past = jnp.where(length > 0.0, ratio * size / length, 0.0)
+            energy = inner(z, image) - past
             length = jnp.where(energy > 0.0, size / energy, 0.0)
+            p = z + ratio * p
+            path = image + ratio * path
             x = x + length * p
-            r = r - length * image
+            r = r - length * path
             z = precondition(r)
-            fresh = inner(r, z)
-            ratio = jnp.where(size > 0.0, fresh / size, 0.0)
-            p = z + ratio * p
-            return (count + 1, again, x, r, p, fresh)
-
-        return lax.while_loop(unfinished, step, (0, 1, x, r, p, size))[2:]
+            return (count + 1, again, x, r, z, p, path, size, length)
+
+        return lax.while_loop(unfinished, step, (0, 1, x, r, z, p, path, before, length))[2:]
 
     start = precondition(right)
-    size = inner(right, start)
-    bound = size[0, 0] * (TOLERANCE * TOLERANCE)
-    zero = jnp.zeros((epochs, width), jnp.float32)
-    coarse = size[0, 0] * (COARSE * COARSE)
-    x, r, p, size = iterate((high, low), MOST_STEPS, coarse, zero, right, start, size)
-    change, left_over, _, _ = iterate((high,), SHORT_STEPS, bound, zero, r, p, size)
+    size = inner(right, start)[0, 0]
+    bound = size * (TOLERANCE * TOLERANCE)
+    coarse = size * (COARSE * COARSE)
+    x, r, z, *rest = iterate(
+        (high, low), MOST_STEPS, coarse, zero, right, start, zero, zero, none, none
+    )
+    size = inner(r, z)
+    change, left_over, *_ = iterate((high,), SHORT_STEPS, bound, zero, r, z, *rest)
     left_over = left_over - products(spread_rows(change), (low,))
     reached = inner(left_over, precondition(left_over))
     unsure = jnp.where(reached[0, 0] <= bound, 0, 1)
 
     def refine(state):
-        _, solved = state
         better = reached < size
         r_now = jnp.where(better, left_over, r)
-        z_now = precondition(r_now)
         solved = iterate(
-            (high, low), MOST_STEPS, bound, solved, r_now, z_now, inner(r_now, z_now)
+            (high, low),
+            MOST_STEPS,
+            bound,
+            state[1],
+            r_now,
+            precondition(r_now),
+            zero,
+            zero,
+            none,
+            none,
         )[0]
         return (0, solved)
 

time: 86.5 us -> 85.7 us (level); the launches traced: 86.2 us -> 86.5 us
  no operation moved by 1% of the time
where the time goes in v7:
time: 85.7 us; the launch traced here: 86.5 us
  blocking collectives  62.4 us (73%)
  Pallas kernels  16.6 us (19%)
  starting transfers between devices  4.94 us (6%)
  waiting for transfers between devices  1.82 us (2%)
    all_to_all x3, blocking collectives, exchange(): lax.all_to_all(x, axis, split_axis=0, concat_axis=0, tiled=True, axis_ind...  62.4 us
    pallas_call x1, Pallas kernels, solve(): pl.pallas_call(solve_kernel, out_shape=[jax.ShapeDtypeStruct((1, width),...  14 us
    ppermute x1, starting transfers between devices, shards(): lax.ppermute(mine, 'sta', [(i, i + 1 - 2 * (i % 2)) for i in range(parts)])  4.94 us
    pallas_call x3, Pallas kernels, call(): pl.pallas_call(kernel, out_shape=pltpu.VMEM(shape, jnp.float32), in_specs...  2.05 us
    ppermute x1, waiting for transfers between devices, shards(): lax.ppermute(mine, 'sta', [(i, i + 1 - 2 * (i % 2)) for i in range(parts)])  1.82 us
  transfers between devices with their start and end apart: 1, of which 1 were waited for; matrix products, arithmetic and copies ran while one was open for 0% of the time, Pallas kernels for 1%

profile of v7, /device:TPU:1, one launch (start us, length us, event | category | flops | bytes accessed | tf_op | source)
XLA Modules:
  0.0 86.5 jit_solution(10724283844154199529)
XLA Ops:
  0.7 1.8 %shard_map.82 = f32[288,1,128]{2,1,0:T(1,128)S(1)} custom-call(s32[1,1]{1,0:T(1,128)S(6)} %copy.13.count_hbm, f32[16]{0:T(128)} %var_hbm.1, bf16[1,1024,256]{2,1,0:T(8,128)(2,1)} %basis_hbm.1, bf16[1,1024]{1,0:T(2,128)(2,1)} %delay_hbm.1, s32[1,1024]{1,0:T(1,128)} %station_hbm.1, f32[1,256]{1,0:T(1,128)} %decay_hbm.1), custom_call_target="tpu_custom_call" | custom-call | tf_op jit(solution)/shard_map/pallas_call | solution.py:317
  2.5 0.0 copy-start
  2.5 0.0 copy-start.1
  2.5 17.4 %all_to_all.16.parts_ref = f32[288,1,128]{2,1,0:T(1,128)S(1)} all-to-all(f32[288,1,128]{2,1,0:T(1,128)S(1)} %shard_map.82), channel_id=1, replica_groups=mesh['tm'=16,'sta'=32] {'sta'}, dimensions={0} | all-to-all | bytes 294912 | tf_op jit(solution)/shard_map/all_to_all | solution.py:352
  19.9 0.1 shard_map.83
  20.0 25.2 %all_to_all.17.rows_ref = f32[144,1,128]{2,1,0:T(1,128)S(1)} all-to-all(f32[144,1,128]{2,1,0:T(1,128)S(1)} %shard_map.83), channel_id=1, replica_groups=mesh['tm'=16,'sta'=32] {'tm'}, dimensions={0} | all-to-all | bytes 147456 | tf_op jit(solution)/shard_map/all_to_all | solution.py:352
  45.2 0.1 shard_map.84
  45.4 19.7 %all_to_all.18.mine_ref = f32[16,144,128]{2,1,0:T(8,128)S(1)} all-to-all(f32[16,144,128]{2,1,0:T(8,128)S(1)} %shard_map.84), channel_id=1, replica_groups={{0,2,4,6,8,10,12,14,16,18,20,22,24,26,28,30},{1,3,5,7,9,11,13,15,17,19,..., dimensions={0} | all-to-all | bytes 2359296 | tf_op jit(solution)/shard_map/all_to_all | solution.py:352
  65.1 4.9 %collective-permute-start = (f32[16,144,128]{2,1,0:T(8,128)S(1)}, f32[16,144,128]{2,1,0:T(8,128)S(1)}, u32[]{:S(2)}, u32[]{:S(2)}) collective-permute-start(f32[16,144,128]{2,1,0:T(8,128)S(1)} %all_to_all.18.mine_ref), channel_id=1, source_target_pairs={{0,1},{1,0},{2,3},{3,2},{4,5},{5,4},{6,7},{7,6},{8,9},{9,8},{10,11... | collective-permute-start | bytes 3538952 | tf_op jit(solution)/shard_map/ppermute | solution.py:397
  70.0 0.0 copy-done
  70.1 0.0 copy-done.1
  70.1 0.6 shard_map.85
  70.7 1.8 %collective-permute-done.other_ref = f32[16,144,128]{2,1,0:T(8,128)S(1)} collective-permute-done((f32[16,144,128]{2,1,0:T(8,128)S(1)}, f32[16,144,128]{2,1,0:T(8,128)S(1)}, u32[]{:S(2)}, u32[]{:S(2)}) %collective-permute-start) | collective-permute-done | bytes 1179680 | tf_op jit(solution)/shard_map/ppermute | solution.py:397
  72.5 14.0 %shard_map.86 = (f32[1,256]{1,0:T(1,128)}, bf16[4096,256]{1,0:T(8,128)(2,1)S(1)}, bf16[4096,256]{1,0:T(8,128)(2,1)S(1)}) custom-call(f32[16,144,128]{2,1,0:T(8,128)S(1)} %collective-permute-done.other_ref, bf16[4096,256]{1,0:T(8,128)(2,1)S(1)} %get-tuple-element.10.high_in, ...), custom_call_target="tpu_custom_call", output_to_operand_aliasing={{1}: (1, {}), {2}: (2, {})} | custom-call | tf_op jit(solution)/shard_map/pallas_call | solution.py:341
Async XLA Ops:
  2.5 67.6 %copy-start = (f32[256]{0:T(256)S(1)}, f32[256]{0:T(256)}, u32[]{:S(2)}) copy-start(f32[256]{0:T(256)} %param.14) | copy-start | bytes 3076
  2.5 67.6 %copy-start.1 = (f32[256]{0:T(256)S(1)}, f32[256]{0:T(256)}, u32[]{:S(2)}) copy-start(f32[256]{0:T(256)} %param.15) | copy-start | bytes 3076
  65.1 7.4 %collective-permute-start = (f32[16,144,128]{2,1,0:T(8,128)S(1)}, f32[16,144,128]{2,1,0:T(8,128)S(1)}, u32[]{:S(2)}, u32[]{:S(2)}) collective-permute-start(f32[16,144,128]{2,1,0:T(8,128)S(1)} %all_to_all.18.mine_ref), channel_id=1, source_target_pairs={{0,1},{1,0},{2,3},{3,2},{4,5},{5,4},{6,7},{7,6},{8,9},{9,8},{10,11... | collective-permute-start | bytes 3538952 | tf_op jit(solution)/shard_map/ppermute | solution.py:397

commit v8 on v7

--- a/solution.py
+++ b/solution.py
@@ -11,8 +11,11 @@
 TOLERANCE = 2e-5
 COARSE = 5e-2
 SHORT_STEPS = 24
+STEEP = 16.0
+ROUNDS = 3
+REDUCTION = 1e-4
 PIECES = 4
-MOST_STEPS = 4000
+MOST_STEPS = 1000
 
 
 def ray_kernel(
@@ -122,23 +125,26 @@
             out_ref[j, epochs * TILE + k : epochs * TILE + k + 1, :] = extra
 
 
-def unpack(slabs_ref, triangles, high, low, epochs, width):
+def whole(slabs_ref, e):
+    place = pl.multiple_of(e * TILE, TILE)
     chips = slabs_ref.shape[0]
+    return jnp.concatenate([slabs_ref[j, pl.ds(place, TILE), :] for j in range(chips)], axis=0)
+
+
+def diagonal_blocks(triangles):
     row = lax.broadcasted_iota(jnp.int32, (HALF, HALF), 0)
     col = lax.broadcasted_iota(jnp.int32, (HALF, HALF), 1)
-
+    turned = triangles.T
+    return (
+        jnp.where(row == col, 0.0, jnp.where(col > row, triangles, turned)),
+        jnp.where(row == col, 0.0, jnp.where(col < row, triangles, turned)),
+    )
+
+
+def unpack(slabs_ref, triangles, high, low, epochs, width):
     def one(e, carry):
-        place = pl.multiple_of(e * TILE, TILE)
-        block = jnp.concatenate(
-            [slabs_ref[j, pl.ds(place, TILE), :] for j in range(chips)], axis=0
-        )
-        turned = block.T
-        pair = (block, turned)
-        if triangles:
-            pair = (
-                jnp.where(row == col, 0.0, jnp.where(col > row, block, turned)),
-                jnp.where(row == col, 0.0, jnp.where(col < row, block, turned)),
-            )
+        block = whole(slabs_ref, e)
+        pair = diagonal_blocks(block) if triangles else (block, block.T)
         for r in range(2):
             rows = pl.ds(pl.multiple_of(e * width + r * HALF, HALF), HALF)
             lane = (r if triangles else 1 - r) * HALF
@@ -173,6 +179,7 @@
     system[1] = link
     system[2] = link_back
     system[3] = right
+    system[4] = diagonal * spread_ref[...]
 
     at = lambda x, e: x[e : e + 1, :]
     ahead = [at(middle, 0)]
@@ -202,7 +209,7 @@
         above = jnp.where(index == e, centre[e], above)
 
 
-def solve_kernel(other_ref, high_in, low_in, response, system, out_ref, high, low):
+def solve_kernel(mine_ref, other_ref, high_in, low_in, response, system, out_ref, high, low):
     epochs, _, width = response.shape
     core = lax.rem(lax.axis_index("sta"), 2)
     epoch_here = lax.axis_index("tm")
@@ -237,13 +244,32 @@
             groups.append(by[:TILE] + by[TILE:])
         return jnp.concatenate(groups, axis=0)
 
-    def apply(p, halves):
-        near = (
+    def near(p):
+        return (
             middle * p
             - link * pltpu.roll(p, epochs - 1, 0)
             - link_back * pltpu.roll(p, 1, 0)
         )
-        return near + products(spread_rows(p), halves)
+
+    def apply(p, halves):
+        return near(p) + products(spread_rows(p), halves)
+
+    def residual(x):
+        def one(e, total):
+            mine = whole(mine_ref, e)
+            other = whole(other_ref, e)
+            corner = jnp.where(core == 0, other, mine)
+            first, second = diagonal_blocks(jnp.where(core == 0, mine, other))
+            kept = jnp.where(index == e, x, 0.0)
+            left, right_half = kept[:, :HALF], kept[:, HALF:]
+            dot = lambda u, m: jnp.dot(
+                u, m, precision=lax.Precision.HIGHEST, preferred_element_type=jnp.float32
+            )
+            lower = dot(left, first) + dot(right_half, corner.T)
+            upper = dot(left, corner) + dot(right_half, second)
+            return total + jnp.concatenate([lower, upper], axis=1)
+
+        return right - near(x) - lax.fori_loop(0, epochs, one, zero)
 
     def inner(a, b):
         return jnp.sum(jnp.sum(a * b, axis=0, keepdims=True), axis=1, keepdims=True)
@@ -284,27 +310,41 @@
     change, left_over, *_ = iterate((high,), SHORT_STEPS, bound, zero, r, z, *rest)
     left_over = left_over - products(spread_rows(change), (low,))
     reached = inner(left_over, precondition(left_over))
-    unsure = jnp.where(reached[0, 0] <= bound, 0, 1)
+    steep = jnp.max(jnp.max(system[4], axis=0, keepdims=True), axis=1, keepdims=True)
+    rounds = jnp.where(reached[0, 0] <= bound, 0, 1)
+    rounds = jnp.where(steep[0, 0] > STEEP, ROUNDS, rounds)
+
+    def correction(r, z, size, goal):
+        def step(state):
+            count, _, x, r, p, size = state
+            image = apply(p, (high, low))
+            energy = inner(p, image)
+            length = jnp.where(energy > 0.0, size / energy, 0.0)
+            x = x + length * p
+            r = r - length * image
+            z = precondition(r)
+            fresh = inner(r, z)
+            p = z + jnp.where(size > 0.0, fresh / size, 0.0) * p
+            return (count + 1, jnp.where(fresh[0, 0] > goal, 1, 0), x, r, p, fresh)
+
+        def unfinished(state):
+            return jnp.logical_and(state[0] < MOST_STEPS, state[1] > 0)
+
+        return lax.while_loop(unfinished, step, (0, 1, zero, r, z, size))[2]
 
     def refine(state):
-        better = reached < size
-        r_now = jnp.where(better, left_over, r)
-        solved = iterate(
-            (high, low),
-            MOST_STEPS,
-            bound,
-            state[1],
-            r_now,
-            precondition(r_now),
-            zero,
-            zero,
-            none,
-            none,
-        )[0]
-        return (0, solved)
-
-    solved = jnp.where(reached < size, x + change, x)
-    solved = lax.while_loop(lambda state: state[0] > 0, refine, (unsure, solved))[1]
+        count, solved = state
+        r = residual(solved)
+        z = precondition(r)
+        size = inner(r, z)
+        goal = jnp.minimum(size[0, 0] * (REDUCTION * REDUCTION), bound)
+        trial = solved + correction(r, z, size, goal)
+        r = residual(trial)
+        solved = jnp.where(inner(r, precondition(r)) < size, trial, solved)
+        return (count - 1, solved)
+
+    solved = jnp.where(reached < size, x + change, jnp.where(size >= 0.0, x, zero))
+    solved = lax.while_loop(lambda state: state[0] > 0, refine, (rounds, solved))[1]
     out_ref[...] = jnp.sum(jnp.where(index == epoch_here, solved, 0.0), axis=0, keepdims=True)
 
 
@@ -328,7 +368,7 @@
     halves = [pltpu.VMEM((epochs * width, width), jnp.bfloat16)] * 2
     tables = [
         pltpu.VMEM((epochs, epochs, width), jnp.float32),
-        pltpu.VMEM((4, epochs, width), jnp.float32),
+        pltpu.VMEM((5, epochs, width), jnp.float32),
     ]
     high, low, response, system = pl.pallas_call(
         prepare_kernel,
@@ -341,11 +381,11 @@
     return pl.pallas_call(
         solve_kernel,
         out_shape=[jax.ShapeDtypeStruct((1, width), jnp.float32)] + halves,
-        in_specs=[VMEM] * 5,
+        in_specs=[VMEM] * 6,
         out_specs=[VMEM] * 3,
-        input_output_aliases={1: 1, 2: 2},
+        input_output_aliases={2: 1, 3: 2},
         compiler_params=pltpu.CompilerParams(vmem_limit_bytes=8 * MIB),
-    )(other, high, low, response, system)[0]
+    )(mine, other, high, low, response, system)[0]
 
 
 def exchange(x, axis, groups=None):

time: 85.7 us -> 83.4 us (0.973); the launches traced: 86.5 us -> 83.1 us
  Pallas kernels: 16.6 us -> 13.3 us
    pallas_call x1, Pallas kernels: 14 us -> 10.6 us  [solve(): pl.pallas_call(solve_kernel, out_shape=[jax.ShapeDtypeStruct((1, width),...]
where the time goes in v8:
time: 83.4 us; the launch traced here: 83.1 us
  blocking collectives  62.4 us (75%)
  Pallas kernels  13.3 us (16%)
  starting transfers between devices  4.94 us (6%)
  waiting for transfers between devices  1.82 us (2%)
    all_to_all x3, blocking collectives, exchange(): lax.all_to_all(x, axis, split_axis=0, concat_axis=0, tiled=True, axis_ind...  62.4 us
    pallas_call x1, Pallas kernels, solve(): pl.pallas_call(solve_kernel, out_shape=[jax.ShapeDtypeStruct((1, width),...  10.6 us
    ppermute x1, starting transfers between devices, shards(): lax.ppermute(mine, 'sta', [(i, i + 1 - 2 * (i % 2)) for i in range(parts)])  4.94 us
    pallas_call x3, Pallas kernels, call(): pl.pallas_call(kernel, out_shape=pltpu.VMEM(shape, jnp.float32), in_specs...  2.05 us
    ppermute x1, waiting for transfers between devices, shards(): lax.ppermute(mine, 'sta', [(i, i + 1 - 2 * (i % 2)) for i in range(parts)])  1.82 us
  transfers between devices with their start and end apart: 1, of which 1 were waited for; matrix products, arithmetic and copies ran while one was open for 0% of the time, Pallas kernels for 1%

profile of v8, /device:TPU:1, one launch (start us, length us, event | category | flops | bytes accessed | tf_op | source)
XLA Modules:
  0.0 83.1 jit_solution(17938400606587558995)
XLA Ops:
  0.7 1.8 %shard_map.82 = f32[288,1,128]{2,1,0:T(1,128)S(1)} custom-call(s32[1,1]{1,0:T(1,128)S(6)} %copy.13.count_hbm, f32[16]{0:T(128)} %var_hbm.1, bf16[1,1024,256]{2,1,0:T(8,128)(2,1)} %basis_hbm.1, bf16[1,1024]{1,0:T(2,128)(2,1)} %delay_hbm.1, s32[1,1024]{1,0:T(1,128)} %station_hbm.1, f32[1,256]{1,0:T(1,128)} %decay_hbm.1), custom_call_target="tpu_custom_call" | custom-call | tf_op jit(solution)/shard_map/pallas_call | solution.py:357
  2.5 0.0 copy-start
  2.5 0.0 copy-start.1
  2.5 17.4 %all_to_all.16.parts_ref = f32[288,1,128]{2,1,0:T(1,128)S(1)} all-to-all(f32[288,1,128]{2,1,0:T(1,128)S(1)} %shard_map.82), channel_id=1, replica_groups=mesh['tm'=16,'sta'=32] {'sta'}, dimensions={0} | all-to-all | bytes 294912 | tf_op jit(solution)/shard_map/all_to_all | solution.py:392
  19.9 0.1 shard_map.83
  20.0 25.2 %all_to_all.17.rows_ref = f32[144,1,128]{2,1,0:T(1,128)S(1)} all-to-all(f32[144,1,128]{2,1,0:T(1,128)S(1)} %shard_map.83), channel_id=1, replica_groups=mesh['tm'=16,'sta'=32] {'tm'}, dimensions={0} | all-to-all | bytes 147456 | tf_op jit(solution)/shard_map/all_to_all | solution.py:392
  45.2 0.1 shard_map.84
  45.4 19.7 %all_to_all.18.mine_ref = f32[16,144,128]{2,1,0:T(8,128)S(1)} all-to-all(f32[16,144,128]{2,1,0:T(8,128)S(1)} %shard_map.84), channel_id=1, replica_groups={{0,2,4,6,8,10,12,14,16,18,20,22,24,26,28,30},{1,3,5,7,9,11,13,15,17,19,..., dimensions={0} | all-to-all | bytes 2359296 | tf_op jit(solution)/shard_map/all_to_all | solution.py:392
  65.1 4.9 %collective-permute-start = (f32[16,144,128]{2,1,0:T(8,128)S(1)}, f32[16,144,128]{2,1,0:T(8,128)S(1)}, u32[]{:S(2)}, u32[]{:S(2)}) collective-permute-start(f32[16,144,128]{2,1,0:T(8,128)S(1)} %all_to_all.18.mine_ref), channel_id=1, source_target_pairs={{0,1},{1,0},{2,3},{3,2},{4,5},{5,4},{6,7},{7,6},{8,9},{9,8},{10,11... | collective-permute-start | bytes 3538952 | tf_op jit(solution)/shard_map/ppermute | solution.py:437
  70.0 0.0 copy-done
  70.1 0.0 copy-done.1
  70.1 0.6 shard_map.85
  70.7 1.8 %collective-permute-done.other_ref = f32[16,144,128]{2,1,0:T(8,128)S(1)} collective-permute-done((f32[16,144,128]{2,1,0:T(8,128)S(1)}, f32[16,144,128]{2,1,0:T(8,128)S(1)}, u32[]{:S(2)}, u32[]{:S(2)}) %collective-permute-start) | collective-permute-done | bytes 1179680 | tf_op jit(solution)/shard_map/ppermute | solution.py:437
  72.5 10.6 %shard_map.86 = (f32[1,256]{1,0:T(1,128)}, bf16[4096,256]{1,0:T(8,128)(2,1)S(1)}, bf16[4096,256]{1,0:T(8,128)(2,1)S(1)}) custom-call(f32[16,144,128]{2,1,0:T(8,128)S(1)} %all_to_all.18.mine_ref, f32[16,144,128]{2,1,0:T(8,128)S(1)} %collective-permute-done.other_ref, ...), custom_call_target="tpu_custom_call", output_to_operand_aliasing={{1}: (2, {}), {2}: (3, {})} | custom-call | tf_op jit(solution)/shard_map/pallas_call | solution.py:381
Async XLA Ops:
  2.5 67.6 %copy-start = (f32[256]{0:T(256)S(1)}, f32[256]{0:T(256)}, u32[]{:S(2)}) copy-start(f32[256]{0:T(256)} %param.14) | copy-start | bytes 3076
  2.5 67.6 %copy-start.1 = (f32[256]{0:T(256)S(1)}, f32[256]{0:T(256)}, u32[]{:S(2)}) copy-start(f32[256]{0:T(256)} %param.15) | copy-start | bytes 3076
  65.1 7.4 %collective-permute-start = (f32[16,144,128]{2,1,0:T(8,128)S(1)}, f32[16,144,128]{2,1,0:T(8,128)S(1)}, u32[]{:S(2)}, u32[]{:S(2)}) collective-permute-start(f32[16,144,128]{2,1,0:T(8,128)S(1)} %all_to_all.18.mine_ref), channel_id=1, source_target_pairs={{0,1},{1,0},{2,3},{3,2},{4,5},{5,4},{6,7},{7,6},{8,9},{9,8},{10,11... | collective-permute-start | bytes 3538952 | tf_op jit(solution)/shard_map/ppermute | solution.py:437

commit v9 on v8

--- a/solution.py
+++ b/solution.py
@@ -8,6 +8,7 @@
 HALF = 128
 TILE = 8
 SLAB = TILE + 1
+EXTRAS = 6
 TOLERANCE = 2e-5
 COARSE = 5e-2
 SHORT_STEPS = 24
@@ -94,12 +95,16 @@
     own = jnp.where(shard == 0, decay_ref[...], 0.0)
     extras = [drive[:, :HALF], drive[:, HALF:], *diagonals, own[:, :HALF], own[:, HALF:]]
     blank = jnp.zeros((1, HALF), jnp.float32)
-    for j in range(HALF // TILE):
-        extra = extras[j] if j < len(extras) else blank
+    chips = HALF // TILE
+    for j in range(chips):
         for c, block in ((0, triangles), (1, corner)):
             base = (2 * j + c) * SLAB
             out_ref[base : base + TILE, 0, :] = block[j * TILE : j * TILE + TILE, :]
-            out_ref[base + TILE, :, :] = extra
+            out_ref[base + TILE, :, :] = blank
+    for k, extra in enumerate(extras):
+        j = lax.rem(lax.axis_index("tm") + k, chips)
+        for c in range(2):
+            out_ref[(2 * j + c) * SLAB + TILE, :, :] = extra
 
 
 def sum_kernel(parts_ref, out_ref):
@@ -116,13 +121,18 @@
 
 
 def copy_kernel(rows_ref, out_ref):
+    chips = out_ref.shape[0]
     epochs = rows_ref.shape[0] // SLAB
-    for k in range(epochs):
-        tile = rows_ref[k * SLAB : k * SLAB + TILE, 0, :]
-        extra = rows_ref[k * SLAB + TILE, :, :]
-        for j in range(out_ref.shape[0]):
+    here = lax.axis_index("sta") // 2
+    tiles = [rows_ref[k * SLAB : k * SLAB + TILE, 0, :] for k in range(epochs)]
+    rows = [
+        rows_ref[lax.rem(here - k + epochs, epochs) * SLAB + TILE, :, :] for k in range(EXTRAS)
+    ]
+    rows.append(jnp.zeros((TILE - EXTRAS, HALF), jnp.float32))
+    tiles.append(jnp.concatenate(rows, axis=0))
+    for j in range(chips):
+        for k, tile in enumerate(tiles):
             out_ref[j, k * TILE : k * TILE + TILE, :] = tile
-            out_ref[j, epochs * TILE + k : epochs * TILE + k + 1, :] = extra
 
 
 def whole(slabs_ref, e):
@@ -162,9 +172,15 @@
     pl.when(core == 0)(lambda: unpack(mine_ref, True, high, low, epochs, width))
     pl.when(core == 1)(lambda: unpack(mine_ref, False, high, low, epochs, width))
 
+    def extra_half(k):
+        row = epochs * TILE + k
+        chips = mine_ref.shape[0]
+        return jnp.concatenate(
+            [mine_ref[(e + k) % chips, row : row + 1, :] for e in range(epochs)], axis=0
+        )
+
     def extra(k):
-        rows = slice(epochs * TILE, epochs * TILE + epochs)
-        return jnp.concatenate([mine_ref[k, rows, :], mine_ref[k + 1, rows, :]], axis=1)
+        return jnp.concatenate([extra_half(k), extra_half(k + 1)], axis=1)
 
     drive, diagonal, decay = extra(0), extra(2), extra(4)
     inverse_noise = 1.0 / ((1.0 - decay * decay) * spread_ref[...])
@@ -402,6 +418,7 @@
     epochs = lax.axis_size("tm")
     parts = lax.axis_size("sta")
     chips = parts // 2
+    tall = (epochs + 1) * TILE
     scratch = [
         pltpu.SMEM((1, 1), jnp.int32),
         pltpu.SMEM((stations,), jnp.float32),
@@ -429,11 +446,11 @@
         sum_kernel, (epochs * SLAB, 1, HALF), [VMEM], [], 4, exchange(share, "sta")
     )
     ours = call(
-        copy_kernel, (chips, epochs * SLAB, HALF), [VMEM], [], 4, exchange(summed, "tm")
+        copy_kernel, (chips, tall, HALF), [VMEM], [], 4, exchange(summed, "tm")
     )
     same_core = [[2 * j + c for j in range(chips)] for c in range(2)]
-    ours = ours.reshape(chips * epochs * SLAB, HALF)
-    mine = exchange(ours, "sta", same_core).reshape(chips, epochs * SLAB, HALF)
+    ours = ours.reshape(chips * tall, HALF)
+    mine = exchange(ours, "sta", same_core).reshape(chips, tall, HALF)
     other = lax.ppermute(mine, "sta", [(i, i + 1 - 2 * (i % 2)) for i in range(parts)])
     return solve(mine, other, mode_variance[None], prior_mean[None], epochs, width)
 

time: 83.4 us -> 114 us (1.37)
  Pallas kernels: 13.3 us -> 44.9 us
    pallas_call x1, Pallas kernels: 10.6 us -> 42.2 us  [solve(): pl.pallas_call(solve_kernel, out_shape=[jax.ShapeDtypeStruct((1, width),...]
where the time goes in v9:
time: 114 us
  blocking collectives  61.5 us (54%)
  Pallas kernels  44.9 us (39%)
  starting transfers between devices  5.13 us (4%)
  waiting for transfers between devices  1.7 us (1%)
    all_to_all x3, blocking collectives, exchange(): lax.all_to_all(x, axis, split_axis=0, concat_axis=0, tiled=True, axis_ind...  61.5 us
    pallas_call x1, Pallas kernels, solve(): pl.pallas_call(solve_kernel, out_shape=[jax.ShapeDtypeStruct((1, width),...  42.2 us
    ppermute x1, starting transfers between devices, shards(): lax.ppermute(mine, 'sta', [(i, i + 1 - 2 * (i % 2)) for i in range(parts)])  5.13 us
  transfers between devices with their start and end apart: 1, of which 1 were waited for; matrix products, arithmetic and copies ran while one was open for 0% of the time, Pallas kernels for 1%

profile of v9, /device:TPU:1, one launch (start us, length us, event | category | flops | bytes accessed | tf_op | source)
XLA Modules:
  0.0 113.9 jit_solution(12556632148821632257)
XLA Ops:
  0.7 1.8 %shard_map.82 = f32[288,1,128]{2,1,0:T(1,128)S(1)} custom-call(s32[1,1]{1,0:T(1,128)S(6)} %copy.13.count_hbm, f32[16]{0:T(128)} %var_hbm.1, bf16[1,1024,256]{2,1,0:T(8,128)(2,1)} %basis_hbm.1, bf16[1,1024]{1,0:T(2,128)(2,1)} %delay_hbm.1, s32[1,1024]{1,0:T(1,128)} %station_hbm.1, f32[1,256]{1,0:T(1,128)} %decay_hbm.1), custom_call_target="tpu_custom_call" | custom-call | tf_op jit(solution)/shard_map/pallas_call | solution.py:373
  2.5 0.0 copy-start
  2.5 0.0 copy-start.1
  2.5 17.4 %all_to_all.16.parts_ref = f32[288,1,128]{2,1,0:T(1,128)S(1)} all-to-all(f32[288,1,128]{2,1,0:T(1,128)S(1)} %shard_map.82), channel_id=1, replica_groups=mesh['tm'=16,'sta'=32] {'sta'}, dimensions={0} | all-to-all | bytes 294912 | tf_op jit(solution)/shard_map/all_to_all | solution.py:408
  19.9 0.1 shard_map.83
  20.0 25.2 %all_to_all.17.rows_ref = f32[144,1,128]{2,1,0:T(1,128)S(1)} all-to-all(f32[144,1,128]{2,1,0:T(1,128)S(1)} %shard_map.83), channel_id=1, replica_groups=mesh['tm'=16,'sta'=32] {'tm'}, dimensions={0} | all-to-all | bytes 147456 | tf_op jit(solution)/shard_map/all_to_all | solution.py:408
  45.2 0.1 shard_map.84
  45.3 18.9 %all_to_all.18.mine_ref = f32[16,136,128]{2,1,0:T(8,128)S(1)} all-to-all(f32[16,136,128]{2,1,0:T(8,128)S(1)} %shard_map.84), channel_id=1, replica_groups={{0,2,4,6,8,10,12,14,16,18,20,22,24,26,28,30},{1,3,5,7,9,11,13,15,17,19,..., dimensions={0} | all-to-all | bytes 2228224 | tf_op jit(solution)/shard_map/all_to_all | solution.py:408
  64.2 5.1 %collective-permute-start = (f32[16,136,128]{2,1,0:T(8,128)S(1)}, f32[16,136,128]{2,1,0:T(8,128)S(1)}, u32[]{:S(2)}, u32[]{:S(2)}) collective-permute-start(f32[16,136,128]{2,1,0:T(8,128)S(1)} %all_to_all.18.mine_ref), channel_id=1, source_target_pairs={{0,1},{1,0},{2,3},{3,2},{4,5},{5,4},{6,7},{7,6},{8,9},{9,8},{10,11... | collective-permute-start | bytes 3342344 | tf_op jit(solution)/shard_map/ppermute | solution.py:454
  69.4 0.0 copy-done
  69.4 0.0 copy-done.1
  69.4 0.6 shard_map.85
  70.0 1.7 %collective-permute-done.other_ref = f32[16,136,128]{2,1,0:T(8,128)S(1)} collective-permute-done((f32[16,136,128]{2,1,0:T(8,128)S(1)}, f32[16,136,128]{2,1,0:T(8,128)S(1)}, u32[]{:S(2)}, u32[]{:S(2)}) %collective-permute-start) | collective-permute-done | bytes 1114144 | tf_op jit(solution)/shard_map/ppermute | solution.py:454
  71.7 42.2 %shard_map.86 = (f32[1,256]{1,0:T(1,128)}, bf16[4096,256]{1,0:T(8,128)(2,1)S(1)}, bf16[4096,256]{1,0:T(8,128)(2,1)S(1)}) custom-call(f32[16,136,128]{2,1,0:T(8,128)S(1)} %all_to_all.18.mine_ref, f32[16,136,128]{2,1,0:T(8,128)S(1)} %collective-permute-done.other_ref, ...), custom_call_target="tpu_custom_call", output_to_operand_aliasing={{1}: (2, {}), {2}: (3, {})} | custom-call | tf_op jit(solution)/shard_map/pallas_call | solution.py:397
Async XLA Ops:
  2.5 66.9 %copy-start = (f32[256]{0:T(256)S(1)}, f32[256]{0:T(256)}, u32[]{:S(2)}) copy-start(f32[256]{0:T(256)} %param.14) | copy-start | bytes 3076
  2.5 66.9 %copy-start.1 = (f32[256]{0:T(256)S(1)}, f32[256]{0:T(256)}, u32[]{:S(2)}) copy-start(f32[256]{0:T(256)} %param.15) | copy-start | bytes 3076
  64.2 7.5 %collective-permute-start = (f32[16,136,128]{2,1,0:T(8,128)S(1)}, f32[16,136,128]{2,1,0:T(8,128)S(1)}, u32[]{:S(2)}, u32[]{:S(2)}) collective-permute-start(f32[16,136,128]{2,1,0:T(8,128)S(1)} %all_to_all.18.mine_ref), channel_id=1, source_target_pairs={{0,1},{1,0},{2,3},{3,2},{4,5},{5,4},{6,7},{7,6},{8,9},{9,8},{10,11... | collective-permute-start | bytes 3342344 | tf_op jit(solution)/shard_map/ppermute | solution.py:454

commit v10 on v9

--- a/solution.py
+++ b/solution.py
@@ -195,7 +195,6 @@
     system[1] = link
     system[2] = link_back
     system[3] = right
-    system[4] = diagonal * spread_ref[...]
 
     at = lambda x, e: x[e : e + 1, :]
     ahead = [at(middle, 0)]
@@ -223,6 +222,15 @@
         above = above * up[e]
         response[e] = response[e] + above
         above = jnp.where(index == e, centre[e], above)
+    start = at(right, 0) * response[0]
+    for e in range(1, epochs):
+        start = start + at(right, e) * response[e]
+    total = jnp.sum(jnp.sum(right * start, axis=0, keepdims=True), axis=1, keepdims=True)
+    peak = jnp.max(
+        jnp.max(diagonal * spread_ref[...], axis=0, keepdims=True), axis=1, keepdims=True
+    )
+    system[4] = start
+    system[5] = jnp.where(index == 0, total, peak)
 
 
 def solve_kernel(mine_ref, other_ref, high_in, low_in, response, system, out_ref, high, low):
@@ -315,8 +323,8 @@
 
         return lax.while_loop(unfinished, step, (0, 1, x, r, z, p, path, before, length))[2:]
 
-    start = precondition(right)
-    size = inner(right, start)[0, 0]
+    start = system[4]
+    size = system[5, 0:1, 0:1][0, 0]
     bound = size * (TOLERANCE * TOLERANCE)
     coarse = size * (COARSE * COARSE)
     x, r, z, *rest = iterate(
@@ -326,7 +334,7 @@
     change, left_over, *_ = iterate((high,), SHORT_STEPS, bound, zero, r, z, *rest)
     left_over = left_over - products(spread_rows(change), (low,))
     reached = inner(left_over, precondition(left_over))
-    steep = jnp.max(jnp.max(system[4], axis=0, keepdims=True), axis=1, keepdims=True)
+    steep = system[5, 1:2, 0:1]
     rounds = jnp.where(reached[0, 0] <= bound, 0, 1)
     rounds = jnp.where(steep[0, 0] > STEEP, ROUNDS, rounds)
 
@@ -384,7 +392,7 @@
     halves = [pltpu.VMEM((epochs * width, width), jnp.bfloat16)] * 2
     tables = [
         pltpu.VMEM((epochs, epochs, width), jnp.float32),
-        pltpu.VMEM((5, epochs, width), jnp.float32),
+        pltpu.VMEM((6, epochs, width), jnp.float32),
     ]
     high, low, response, system = pl.pallas_call(
         prepare_kernel,

time: 114 us -> 83.8 us (0.74)
  Pallas kernels: 44.9 us -> 14.5 us
    pallas_call x1, Pallas kernels: 42.2 us -> 11.8 us  [solve(): pl.pallas_call(solve_kernel, out_shape=[jax.ShapeDtypeStruct((1, width),...]
where the time goes in v10:
time: 83.8 us; the launch traced here: 83.5 us
  blocking collectives  61.5 us (73%)
  Pallas kernels  14.5 us (17%)
  starting transfers between devices  5.13 us (6%)
  waiting for transfers between devices  1.6 us (2%)
    all_to_all x3, blocking collectives, exchange(): lax.all_to_all(x, axis, split_axis=0, concat_axis=0, tiled=True, axis_ind...  61.5 us
    pallas_call x1, Pallas kernels, solve(): pl.pallas_call(solve_kernel, out_shape=[jax.ShapeDtypeStruct((1, width),...  11.8 us
    ppermute x1, starting transfers between devices, shards(): lax.ppermute(mine, 'sta', [(i, i + 1 - 2 * (i % 2)) for i in range(parts)])  5.13 us
    pallas_call x3, Pallas kernels, call(): pl.pallas_call(kernel, out_shape=pltpu.VMEM(shape, jnp.float32), in_specs...  1.98 us
  transfers between devices with their start and end apart: 1, of which 1 were waited for; matrix products, arithmetic and copies ran while one was open for 0% of the time, Pallas kernels for 1%

profile of v10, /device:TPU:1, one launch (start us, length us, event | category | flops | bytes accessed | tf_op | source)
XLA Modules:
  0.0 83.5 jit_solution(601892451783005445)
XLA Ops:
  0.7 1.8 %shard_map.82 = f32[288,1,128]{2,1,0:T(1,128)S(1)} custom-call(s32[1,1]{1,0:T(1,128)S(6)} %copy.13.count_hbm, f32[16]{0:T(128)} %var_hbm.1, bf16[1,1024,256]{2,1,0:T(8,128)(2,1)} %basis_hbm.1, bf16[1,1024]{1,0:T(2,128)(2,1)} %delay_hbm.1, s32[1,1024]{1,0:T(1,128)} %station_hbm.1, f32[1,256]{1,0:T(1,128)} %decay_hbm.1), custom_call_target="tpu_custom_call" | custom-call | tf_op jit(solution)/shard_map/pallas_call | solution.py:381
  2.5 0.0 copy-start
  2.5 0.0 copy-start.1
  2.5 17.4 %all_to_all.16.parts_ref = f32[288,1,128]{2,1,0:T(1,128)S(1)} all-to-all(f32[288,1,128]{2,1,0:T(1,128)S(1)} %shard_map.82), channel_id=1, replica_groups=mesh['tm'=16,'sta'=32] {'sta'}, dimensions={0} | all-to-all | bytes 294912 | tf_op jit(solution)/shard_map/all_to_all | solution.py:416
  19.9 0.1 shard_map.83
  20.0 25.2 %all_to_all.17.rows_ref = f32[144,1,128]{2,1,0:T(1,128)S(1)} all-to-all(f32[144,1,128]{2,1,0:T(1,128)S(1)} %shard_map.83), channel_id=1, replica_groups=mesh['tm'=16,'sta'=32] {'tm'}, dimensions={0} | all-to-all | bytes 147456 | tf_op jit(solution)/shard_map/all_to_all | solution.py:416
  45.2 0.1 shard_map.84
  45.3 18.9 %all_to_all.18.mine_ref = f32[16,136,128]{2,1,0:T(8,128)S(1)} all-to-all(f32[16,136,128]{2,1,0:T(8,128)S(1)} %shard_map.84), channel_id=1, replica_groups={{0,2,4,6,8,10,12,14,16,18,20,22,24,26,28,30},{1,3,5,7,9,11,13,15,17,19,..., dimensions={0} | all-to-all | bytes 2228224 | tf_op jit(solution)/shard_map/all_to_all | solution.py:416
  64.2 5.1 %collective-permute-start = (f32[16,136,128]{2,1,0:T(8,128)S(1)}, f32[16,136,128]{2,1,0:T(8,128)S(1)}, u32[]{:S(2)}, u32[]{:S(2)}) collective-permute-start(f32[16,136,128]{2,1,0:T(8,128)S(1)} %all_to_all.18.mine_ref), channel_id=1, source_target_pairs={{0,1},{1,0},{2,3},{3,2},{4,5},{5,4},{6,7},{7,6},{8,9},{9,8},{10,11... | collective-permute-start | bytes 3342344 | tf_op jit(solution)/shard_map/ppermute | solution.py:462
  69.4 0.0 copy-done
  69.4 0.0 copy-done.1
  69.4 0.7 shard_map.85
  70.1 1.6 %collective-permute-done.other_ref = f32[16,136,128]{2,1,0:T(8,128)S(1)} collective-permute-done((f32[16,136,128]{2,1,0:T(8,128)S(1)}, f32[16,136,128]{2,1,0:T(8,128)S(1)}, u32[]{:S(2)}, u32[]{:S(2)}) %collective-permute-start) | collective-permute-done | bytes 1114144 | tf_op jit(solution)/shard_map/ppermute | solution.py:462
  71.7 11.8 %shard_map.86 = (f32[1,256]{1,0:T(1,128)}, bf16[4096,256]{1,0:T(8,128)(2,1)S(1)}, bf16[4096,256]{1,0:T(8,128)(2,1)S(1)}) custom-call(f32[16,136,128]{2,1,0:T(8,128)S(1)} %all_to_all.18.mine_ref, f32[16,136,128]{2,1,0:T(8,128)S(1)} %collective-permute-done.other_ref, ...), custom_call_target="tpu_custom_call", output_to_operand_aliasing={{1}: (2, {}), {2}: (3, {})} | custom-call | tf_op jit(solution)/shard_map/pallas_call | solution.py:405
Async XLA Ops:
  2.5 66.9 %copy-start = (f32[256]{0:T(256)S(1)}, f32[256]{0:T(256)}, u32[]{:S(2)}) copy-start(f32[256]{0:T(256)} %param.14) | copy-start | bytes 3076
  2.5 66.9 %copy-start.1 = (f32[256]{0:T(256)S(1)}, f32[256]{0:T(256)}, u32[]{:S(2)}) copy-start(f32[256]{0:T(256)} %param.15) | copy-start | bytes 3076
  64.2 7.5 %collective-permute-start = (f32[16,136,128]{2,1,0:T(8,128)S(1)}, f32[16,136,128]{2,1,0:T(8,128)S(1)}, u32[]{:S(2)}, u32[]{:S(2)}) collective-permute-start(f32[16,136,128]{2,1,0:T(8,128)S(1)} %all_to_all.18.mine_ref), channel_id=1, source_target_pairs={{0,1},{1,0},{2,3},{3,2},{4,5},{5,4},{6,7},{7,6},{8,9},{9,8},{10,11... | collective-permute-start | bytes 3342344 | tf_op jit(solution)/shard_map/ppermute | solution.py:462
